TPU v7x, 128 devices: a whole 4x4x4 slice. The times are simulated.
128 devices in a mesh: ctx: 16 (over x_hi, z, core), tp: 8 (over y, x_lo).
Axes of the slice: x: 4 (x_hi: 2, x_lo: 2; x = x_hi * 2 + x_lo), y: 4, z: 4, core: 2. Of those that a mesh axis runs over, the one named last changes fastest.
Arguments:
- queries: bfloat16 [2048, 4096], P('ctx', 'tp'), may hold values from -7 to 7
- key_cache: bfloat16 [32768, 1024], P('ctx', 'tp'), may hold values from -7 to 7
- value_cache: bfloat16 [32768, 1024], P('ctx', 'tp'), may hold values from -6 to 6
- scale_exps: int32 [2, 8], P(None, 'tp'), may hold values from -1 to 1
- query_pos: int32 [2048], replicated, may hold values from 30720 to 32767, as said below
- key_pos: int32 [32768], P('ctx'), may hold values from 0 to 32767, as said below
- resid: bfloat16 [2048, 4096], P('ctx'), may hold values from -0.5 to 0.5
- out_weight: bfloat16 [4096, 4096], P('tp'), may hold values from -0.09375 to 0.09375
- norm_gain: bfloat16 [4096], replicated, may hold values from 0.5 to 1.5
- gate_weight: bfloat16 [4096, 14336], P('ctx', 'tp'), may hold values from -0.09375 to 0.09375
- up_weight: bfloat16 [4096, 14336], P('ctx', 'tp'), may hold values from -0.09375 to 0.09375
Outputs:
- activated: bfloat16 [2048, 14336], P('ctx', 'tp')
Inputs may be any that keep to these rules, and one draw needn't show every extreme that they name: `key_pos`: every position 0 to 32767 stands once. `query_pos`: every position 30720 to 32767 stands once.
All inputs are finite; a program needn't handle non-finite values.
Results may differ from a plain program's by a relative error of at most 0.025.
Values may be sent and summed in bfloat16 or wider, within the bound.
A program may use at most 128 MiB of HBM per device.

v0:
```python
import math

import jax
import jax.numpy as jnp
from jax import lax
from jax.sharding import PartitionSpec as P

HD = 128


def shifted(value, axis, steps):
    count = lax.axis_size(axis)
    pairs = [(source, (source + steps) % count) for source in range(count)]
    return lax.ppermute(value, axis, pairs)


def block_partial(
    query_block, query_places, key_heads, value_heads, key_places, key_factor, value_factor
):
    scores = jnp.einsum(
        "qhgd,khd->hqgk", query_block, key_heads, preferred_element_type=jnp.float32
    )
    scores = scores * key_factor[:, None, None, None]
    visible = key_places[None, None, None, :] <= query_places[None, :, None, None]
    block_max = jnp.max(jnp.where(visible, scores, -1e30), axis=-1)
    weights = jnp.where(visible, jnp.exp(scores - block_max[..., None]), 0.0)
    block_total = jnp.sum(weights, axis=-1)
    block_out = jnp.einsum(
        "hqgk,khd->qhgd",
        weights.astype(jnp.bfloat16),
        value_heads,
        preferred_element_type=jnp.float32,
    )
    block_out = block_out * value_factor[None, :, None, None]
    return (block_out, block_max.transpose(1, 0, 2), block_total.transpose(1, 0, 2))


def merge_partials(earlier, later):
    highest = jnp.maximum(earlier[1], later[1])
    keep_old = jnp.exp(earlier[1] - highest)
    keep_new = jnp.exp(later[1] - highest)
    merged_out = earlier[0] * keep_old[..., None] + later[0] * keep_new[..., None]
    merged_total = earlier[2] * keep_old + later[2] * keep_new
    return (merged_out, highest, merged_total)


def body(
    queries,
    key_cache,
    value_cache,
    scale_exps,
    query_pos,
    key_pos,
    resid,
    out_weight,
    norm_gain,
    gate_weight,
    up_weight,
):
    row_count = queries.shape[0]
    heads_here = queries.shape[1] // HD
    kv_here = key_cache.shape[1] // HD
    group_size = heads_here // kv_here
    cache_rows = key_cache.shape[0]
    ctx_count = lax.axis_size("ctx")
    own_index = lax.axis_index("ctx")
    key_heads = key_cache.reshape(cache_rows, kv_here, HD)
    value_heads = value_cache.reshape(cache_rows, kv_here, HD)
    key_factor = jnp.exp2(scale_exps[0].astype(jnp.float32)) / math.sqrt(HD)
    value_factor = jnp.exp2(scale_exps[1].astype(jnp.float32))
    query_heads = queries.reshape(row_count, kv_here, group_size, HD)

    def partial_for(query_block, owner_index):
        places = lax.dynamic_slice_in_dim(query_pos, owner_index * row_count, row_count, 0)
        return block_partial(
            query_block, places, key_heads, value_heads, key_pos, key_factor, value_factor
        )

    def visit(turn_index, state):
        query_block, carried = state
        owner_index = (own_index - turn_index) % ctx_count
        carried = merge_partials(carried, partial_for(query_block, owner_index))
        query_block = shifted(query_block, "ctx", 1)
        carried = shifted((carried[0], carried[1], carried[2]), "ctx", 1)
        return (query_block, carried)

    start_state = (
        jnp.zeros((row_count, kv_here, group_size, HD), jnp.float32),
        jnp.full((row_count, kv_here, group_size), -1e30, jnp.float32),
        jnp.zeros((row_count, kv_here, group_size), jnp.float32),
    )
    query_block, carried = lax.fori_loop(0, ctx_count - 1, visit, (query_heads, start_state))
    last_owner = (own_index - (ctx_count - 1)) % ctx_count
    carried = merge_partials(carried, partial_for(query_block, last_owner))
    final_out, final_max, final_total = (
        shifted(carried[0].astype(jnp.bfloat16), "ctx", 1).astype(jnp.float32),
        shifted(carried[1].astype(jnp.bfloat16), "ctx", 1).astype(jnp.float32),
        shifted(carried[2].astype(jnp.bfloat16), "ctx", 1).astype(jnp.float32),
    )
    attention = (
        (final_out / final_total[..., None])
        .astype(jnp.bfloat16)
        .reshape(row_count, heads_here * HD)
    )
    projected = jnp.dot(attention, out_weight, preferred_element_type=jnp.float32)
    summed = lax.psum(projected.astype(jnp.bfloat16), "tp").astype(jnp.float32)
    stream = resid.astype(jnp.float32) + summed
    mean_square = jnp.mean(stream * stream, axis=-1, keepdims=True)
    normed = (stream * lax.rsqrt(mean_square + 1e-05) * norm_gain.astype(jnp.float32)).astype(
        jnp.bfloat16
    )
    gate = jnp.dot(
        normed,
        lax.all_gather(gate_weight, "ctx", axis=0, tiled=True),
        preferred_element_type=jnp.float32,
    )
    up_part = jnp.dot(
        normed,
        lax.all_gather(up_weight, "ctx", axis=0, tiled=True),
        preferred_element_type=jnp.float32,
    )
    return (jax.nn.silu(gate) * up_part).astype(jnp.bfloat16)


def solution(mesh):
    placed = (
        P("ctx", "tp"),
        P("ctx", "tp"),
        P("ctx", "tp"),
        P(None, "tp"),
        P(),
        P("ctx"),
        P("ctx", None),
        P("tp", None),
        P(),
        P("ctx", "tp"),
        P("ctx", "tp"),
    )
    return jax.shard_map(
        body, mesh=mesh, in_specs=placed, out_specs=P("ctx", "tp"), check_vma=False
    )
```

profile of v0, /device:TPU:1, one launch (start us, length us, event | category | flops | bytes accessed | tf_op | source)
XLA Modules:
  0.0 508.0 jit_solution(6294812821972166625)
XLA Ops:
  13.0 249.5 %while.21 = (s32[]{:T(128)}, bf16[128,1,4,128]{3,0,2,1:T(8,128)(2,1)S(1)}, f32[128,1,4,128]{3,0,2,1:T(8,128)S(1)}, f32[128,1,4]{0,2,1:T(4,128)S(1)}, f32[128,1,4...) while((s32[]{:T(128)}, ...), condition=%wide.region_3.4_spmd, body=%wide.region_0.3_spmd.sunk | while | flops 548931584 | bytes 19322908 | solution.py:92
  52.4 4.5 collective-permute-done.2
  63.2 5.9 %collective-permute-start.2 = (f32[128,1,4]{0,2,1:T(4,128)S(1)}, f32[128,1,4]{0,2,1:T(4,128)S(1)}, u32[]{:S(2)}, u32[]{:S(2)}) collective-permute-start(f32[128,1,4]{0,2,1:T(4,128)S(1)} %get-tuple-element.431), channel_id=1, source_target_pairs={{0,8},{8,16},{16,24},{24,32},{32,40},{40,48},{48,56},{56,64},{64,7... | collective-permute-start | bytes 6152 | tf_op jit(solution)/shard_map/while/body/eval_jaxpr/ppermute | solution.py:14
  69.5 4.5 collective-permute-done.2
  80.3 5.9 %collective-permute-start.2 = (f32[128,1,4]{0,2,1:T(4,128)S(1)}, f32[128,1,4]{0,2,1:T(4,128)S(1)}, u32[]{:S(2)}, u32[]{:S(2)}) collective-permute-start(f32[128,1,4]{0,2,1:T(4,128)S(1)} %get-tuple-element.431), channel_id=1, source_target_pairs={{0,8},{8,16},{16,24},{24,32},{32,40},{40,48},{48,56},{56,64},{64,7... | collective-permute-start | bytes 6152 | tf_op jit(solution)/shard_map/while/body/eval_jaxpr/ppermute | solution.py:14
  86.6 4.5 collective-permute-done.2
  97.5 5.9 %collective-permute-start.2 = (f32[128,1,4]{0,2,1:T(4,128)S(1)}, f32[128,1,4]{0,2,1:T(4,128)S(1)}, u32[]{:S(2)}, u32[]{:S(2)}) collective-permute-start(f32[128,1,4]{0,2,1:T(4,128)S(1)} %get-tuple-element.431), channel_id=1, source_target_pairs={{0,8},{8,16},{16,24},{24,32},{32,40},{40,48},{48,56},{56,64},{64,7... | collective-permute-start | bytes 6152 | tf_op jit(solution)/shard_map/while/body/eval_jaxpr/ppermute | solution.py:14
  103.8 4.5 collective-permute-done.2
  114.6 5.9 %collective-permute-start.2 = (f32[128,1,4]{0,2,1:T(4,128)S(1)}, f32[128,1,4]{0,2,1:T(4,128)S(1)}, u32[]{:S(2)}, u32[]{:S(2)}) collective-permute-start(f32[128,1,4]{0,2,1:T(4,128)S(1)} %get-tuple-element.431), channel_id=1, source_target_pairs={{0,8},{8,16},{16,24},{24,32},{32,40},{40,48},{48,56},{56,64},{64,7... | collective-permute-start | bytes 6152 | tf_op jit(solution)/shard_map/while/body/eval_jaxpr/ppermute | solution.py:14
  120.9 4.5 collective-permute-done.2
  131.8 5.9 %collective-permute-start.2 = (f32[128,1,4]{0,2,1:T(4,128)S(1)}, f32[128,1,4]{0,2,1:T(4,128)S(1)}, u32[]{:S(2)}, u32[]{:S(2)}) collective-permute-start(f32[128,1,4]{0,2,1:T(4,128)S(1)} %get-tuple-element.431), channel_id=1, source_target_pairs={{0,8},{8,16},{16,24},{24,32},{32,40},{40,48},{48,56},{56,64},{64,7... | collective-permute-start | bytes 6152 | tf_op jit(solution)/shard_map/while/body/eval_jaxpr/ppermute | solution.py:14
  138.0 4.5 collective-permute-done.2
  148.9 5.9 %collective-permute-start.2 = (f32[128,1,4]{0,2,1:T(4,128)S(1)}, f32[128,1,4]{0,2,1:T(4,128)S(1)}, u32[]{:S(2)}, u32[]{:S(2)}) collective-permute-start(f32[128,1,4]{0,2,1:T(4,128)S(1)} %get-tuple-element.431), channel_id=1, source_target_pairs={{0,8},{8,16},{16,24},{24,32},{32,40},{40,48},{48,56},{56,64},{64,7... | collective-permute-start | bytes 6152 | tf_op jit(solution)/shard_map/while/body/eval_jaxpr/ppermute | solution.py:14
  155.2 4.5 collective-permute-done.2
  166.0 5.9 %collective-permute-start.2 = (f32[128,1,4]{0,2,1:T(4,128)S(1)}, f32[128,1,4]{0,2,1:T(4,128)S(1)}, u32[]{:S(2)}, u32[]{:S(2)}) collective-permute-start(f32[128,1,4]{0,2,1:T(4,128)S(1)} %get-tuple-element.431), channel_id=1, source_target_pairs={{0,8},{8,16},{16,24},{24,32},{32,40},{40,48},{48,56},{56,64},{64,7... | collective-permute-start | bytes 6152 | tf_op jit(solution)/shard_map/while/body/eval_jaxpr/ppermute | solution.py:14
  172.3 4.5 collective-permute-done.2
  183.2 5.9 %collective-permute-start.2 = (f32[128,1,4]{0,2,1:T(4,128)S(1)}, f32[128,1,4]{0,2,1:T(4,128)S(1)}, u32[]{:S(2)}, u32[]{:S(2)}) collective-permute-start(f32[128,1,4]{0,2,1:T(4,128)S(1)} %get-tuple-element.431), channel_id=1, source_target_pairs={{0,8},{8,16},{16,24},{24,32},{32,40},{40,48},{48,56},{56,64},{64,7... | collective-permute-start | bytes 6152 | tf_op jit(solution)/shard_map/while/body/eval_jaxpr/ppermute | solution.py:14
  189.5 4.5 collective-permute-done.2
  200.3 5.9 %collective-permute-start.2 = (f32[128,1,4]{0,2,1:T(4,128)S(1)}, f32[128,1,4]{0,2,1:T(4,128)S(1)}, u32[]{:S(2)}, u32[]{:S(2)}) collective-permute-start(f32[128,1,4]{0,2,1:T(4,128)S(1)} %get-tuple-element.431), channel_id=1, source_target_pairs={{0,8},{8,16},{16,24},{24,32},{32,40},{40,48},{48,56},{56,64},{64,7... | collective-permute-start | bytes 6152 | tf_op jit(solution)/shard_map/while/body/eval_jaxpr/ppermute | solution.py:14
  206.6 4.5 collective-permute-done.2
  217.4 5.9 %collective-permute-start.2 = (f32[128,1,4]{0,2,1:T(4,128)S(1)}, f32[128,1,4]{0,2,1:T(4,128)S(1)}, u32[]{:S(2)}, u32[]{:S(2)}) collective-permute-start(f32[128,1,4]{0,2,1:T(4,128)S(1)} %get-tuple-element.431), channel_id=1, source_target_pairs={{0,8},{8,16},{16,24},{24,32},{32,40},{40,48},{48,56},{56,64},{64,7... | collective-permute-start | bytes 6152 | tf_op jit(solution)/shard_map/while/body/eval_jaxpr/ppermute | solution.py:14
  223.7 4.5 collective-permute-done.2
  234.6 5.9 %collective-permute-start.2 = (f32[128,1,4]{0,2,1:T(4,128)S(1)}, f32[128,1,4]{0,2,1:T(4,128)S(1)}, u32[]{:S(2)}, u32[]{:S(2)}) collective-permute-start(f32[128,1,4]{0,2,1:T(4,128)S(1)} %get-tuple-element.431), channel_id=1, source_target_pairs={{0,8},{8,16},{16,24},{24,32},{32,40},{40,48},{48,56},{56,64},{64,7... | collective-permute-start | bytes 6152 | tf_op jit(solution)/shard_map/while/body/eval_jaxpr/ppermute | solution.py:14
  240.9 4.5 collective-permute-done.2
  251.7 5.9 %collective-permute-start.2 = (f32[128,1,4]{0,2,1:T(4,128)S(1)}, f32[128,1,4]{0,2,1:T(4,128)S(1)}, u32[]{:S(2)}, u32[]{:S(2)}) collective-permute-start(f32[128,1,4]{0,2,1:T(4,128)S(1)} %get-tuple-element.431), channel_id=1, source_target_pairs={{0,8},{8,16},{16,24},{24,32},{32,40},{40,48},{48,56},{56,64},{64,7... | collective-permute-start | bytes 6152 | tf_op jit(solution)/shard_map/while/body/eval_jaxpr/ppermute | solution.py:14
  258.0 4.5 collective-permute-done.2
  266.8 9.2 %collective-permute-done.5 = bf16[128,1,4]{0,2,1:T(4,128)(2,1)S(1)} collective-permute-done((bf16[128,1,4]{0,2,1:T(4,128)(2,1)S(1)}, bf16[128,1,4]{0,2,1:T(4,128)(2,1)S(1)}, u32[]{:S(2)}, u32[]{:S(2)}) %collective-permute-start.5) | collective-permute-done | bytes 1056 | tf_op jit(solution)/shard_map/ppermute | solution.py:14
  277.5 4.0 convolution_convert_fusion
  282.8 137.4 %all-reduce.2.cloned.1.call-done = bf16[128,4096]{1,0:T(8,128)(2,1)} async-done(((bf16[128,4096]{1,0:T(8,128)(2,1)}), bf16[128,4096]{1,0:T(8,128)(2,1)}) %all-reduce.2.cloned.1.call-update) | async-done | bytes 1048592 | tf_op jit(solution)/shard_map/psum | solution.py:106
  421.9 7.8 %fusion.64 = f32[128,1792]{1,0:T(8,128)S(1)} fusion(bf16[4096,1792]{1,0:T(8,128)(2,1)} %all-gather.3.cloned.1.call-done, bf16[128,4096]{1,0:T(8,128)(2,1)} %all-reduce.2.cloned.1.call-done, bf16[128,4096]{1,0:T(8,128)(2,1)S(1)} %copy-done, f32[4096]{0:T(1024)S(1)} %convert_element_type.64, f32[128]{0:T(128)S(1)} %add_rsqrt_fusion), kind=kOutput, calls=%fused_computation.61 | convolution fusion | flops 1882193920 | bytes 17711616 | tf_op jit(solution)/shard_map/dot_general | solution.py:112
  429.7 62.6 %all-gather.5.cloned.1.call-done = bf16[4096,1792]{1,0:T(8,128)(2,1)} async-done(((bf16[256,1792]{1,0:T(8,128)(2,1)}), bf16[4096,1792]{1,0:T(8,128)(2,1)}) %all-gather.5.cloned.1.call-update) | async-done | bytes 14680080 | tf_op jit(solution)/shard_map/all_gather | solution.py:119
  492.2 8.3 %fusion.31 = bf16[128,1792]{1,0:T(8,128)(2,1)} fusion(bf16[4096,1792]{1,0:T(8,128)(2,1)} %all-gather.5.cloned.1.call-done, f32[128,1792]{1,0:T(8,128)S(1)} %fusion.64, bf16[128,4096]{1,0:T(8,128)(2,1)S(1)} %copy-done.1, bf16[128,4096]{1,0:T(8,128)(2,1)S(1)} %copy-done, f32[4096]{0:T(1024)S(1)} %convert_element_type.64, f32[128]{0:T(128)S(1)} %add_rsqrt_fusion), kind=kOutput, calls=%fused_computation.31 | convolution fusion | flops 1883570176 | bytes 18170368 | tf_op jit(solution)/shard_map/dot_general | solution.py:117
  (266 shorter events, 131.5 us)
Async XLA Ops:
  7.4 412.8 %all-reduce.2.cloned.1.call-start = ((), (), s32[]{:S(2)}) async-start(), calls=%async_computation | async-start | bytes 2097152 | tf_op jit(solution)/shard_map/psum | solution.py:106
  63.0 10.9 %collective-permute-start.1 = (f32[128,1,4,128]{3,0,2,1:T(8,128)S(1)}, f32[128,1,4,128]{3,0,2,1:T(8,128)S(1)}, u32[]{:S(2)}, u32[]{:S(2)}) collective-permute-start(f32[128,1,4,128]{3,0,2,1:T(8,128)S(1)} %fusion.79), channel_id=1, source_target_pairs={{0,8},{8,16},{16,24},{24,32},{32,40},{40,48},{48,56},{56,64},{64,7... | collective-permute-start | bytes 786440 | tf_op jit(solution)/shard_map/while/body/eval_jaxpr/ppermute | solution.py:14
  63.1 10.8 %collective-permute-start = (bf16[128,1,4,128]{3,0,2,1:T(8,128)(2,1)S(1)}, bf16[128,1,4,128]{3,0,2,1:T(8,128)(2,1)S(1)}, u32[]{:S(2)}, u32[]{:S(2)}) collective-permute-start(bf16[128,1,4,128]{3,0,2,1:T(8,128)(2,1)S(1)} %copy.21), channel_id=1, source_target_pairs={{0,8},{8,16},{16,24},{24,32},{32,40},{40,48},{48,56},{56,64},{64,7... | collective-permute-start | bytes 393224 | tf_op jit(solution)/shard_map/while/body/eval_jaxpr/ppermute | solution.py:14
  63.2 10.7 %collective-permute-start.2 = (f32[128,1,4]{0,2,1:T(4,128)S(1)}, f32[128,1,4]{0,2,1:T(4,128)S(1)}, u32[]{:S(2)}, u32[]{:S(2)}) collective-permute-start(f32[128,1,4]{0,2,1:T(4,128)S(1)} %get-tuple-element.431), channel_id=1, source_target_pairs={{0,8},{8,16},{16,24},{24,32},{32,40},{40,48},{48,56},{56,64},{64,7... | collective-permute-start | bytes 6152 | tf_op jit(solution)/shard_map/while/body/eval_jaxpr/ppermute | solution.py:14
  80.2 10.9 %collective-permute-start.1 = (f32[128,1,4,128]{3,0,2,1:T(8,128)S(1)}, f32[128,1,4,128]{3,0,2,1:T(8,128)S(1)}, u32[]{:S(2)}, u32[]{:S(2)}) collective-permute-start(f32[128,1,4,128]{3,0,2,1:T(8,128)S(1)} %fusion.79), channel_id=1, source_target_pairs={{0,8},{8,16},{16,24},{24,32},{32,40},{40,48},{48,56},{56,64},{64,7... | collective-permute-start | bytes 786440 | tf_op jit(solution)/shard_map/while/body/eval_jaxpr/ppermute | solution.py:14
  80.3 10.8 %collective-permute-start = (bf16[128,1,4,128]{3,0,2,1:T(8,128)(2,1)S(1)}, bf16[128,1,4,128]{3,0,2,1:T(8,128)(2,1)S(1)}, u32[]{:S(2)}, u32[]{:S(2)}) collective-permute-start(bf16[128,1,4,128]{3,0,2,1:T(8,128)(2,1)S(1)} %copy.21), channel_id=1, source_target_pairs={{0,8},{8,16},{16,24},{24,32},{32,40},{40,48},{48,56},{56,64},{64,7... | collective-permute-start | bytes 393224 | tf_op jit(solution)/shard_map/while/body/eval_jaxpr/ppermute | solution.py:14
  80.3 10.7 %collective-permute-start.2 = (f32[128,1,4]{0,2,1:T(4,128)S(1)}, f32[128,1,4]{0,2,1:T(4,128)S(1)}, u32[]{:S(2)}, u32[]{:S(2)}) collective-permute-start(f32[128,1,4]{0,2,1:T(4,128)S(1)} %get-tuple-element.431), channel_id=1, source_target_pairs={{0,8},{8,16},{16,24},{24,32},{32,40},{40,48},{48,56},{56,64},{64,7... | collective-permute-start | bytes 6152 | tf_op jit(solution)/shard_map/while/body/eval_jaxpr/ppermute | solution.py:14
  97.3 10.9 %collective-permute-start.1 = (f32[128,1,4,128]{3,0,2,1:T(8,128)S(1)}, f32[128,1,4,128]{3,0,2,1:T(8,128)S(1)}, u32[]{:S(2)}, u32[]{:S(2)}) collective-permute-start(f32[128,1,4,128]{3,0,2,1:T(8,128)S(1)} %fusion.79), channel_id=1, source_target_pairs={{0,8},{8,16},{16,24},{24,32},{32,40},{40,48},{48,56},{56,64},{64,7... | collective-permute-start | bytes 786440 | tf_op jit(solution)/shard_map/while/body/eval_jaxpr/ppermute | solution.py:14
  97.4 10.8 %collective-permute-start = (bf16[128,1,4,128]{3,0,2,1:T(8,128)(2,1)S(1)}, bf16[128,1,4,128]{3,0,2,1:T(8,128)(2,1)S(1)}, u32[]{:S(2)}, u32[]{:S(2)}) collective-permute-start(bf16[128,1,4,128]{3,0,2,1:T(8,128)(2,1)S(1)} %copy.21), channel_id=1, source_target_pairs={{0,8},{8,16},{16,24},{24,32},{32,40},{40,48},{48,56},{56,64},{64,7... | collective-permute-start | bytes 393224 | tf_op jit(solution)/shard_map/while/body/eval_jaxpr/ppermute | solution.py:14
  97.5 10.7 %collective-permute-start.2 = (f32[128,1,4]{0,2,1:T(4,128)S(1)}, f32[128,1,4]{0,2,1:T(4,128)S(1)}, u32[]{:S(2)}, u32[]{:S(2)}) collective-permute-start(f32[128,1,4]{0,2,1:T(4,128)S(1)} %get-tuple-element.431), channel_id=1, source_target_pairs={{0,8},{8,16},{16,24},{24,32},{32,40},{40,48},{48,56},{56,64},{64,7... | collective-permute-start | bytes 6152 | tf_op jit(solution)/shard_map/while/body/eval_jaxpr/ppermute | solution.py:14
  114.5 10.9 %collective-permute-start.1 = (f32[128,1,4,128]{3,0,2,1:T(8,128)S(1)}, f32[128,1,4,128]{3,0,2,1:T(8,128)S(1)}, u32[]{:S(2)}, u32[]{:S(2)}) collective-permute-start(f32[128,1,4,128]{3,0,2,1:T(8,128)S(1)} %fusion.79), channel_id=1, source_target_pairs={{0,8},{8,16},{16,24},{24,32},{32,40},{40,48},{48,56},{56,64},{64,7... | collective-permute-start | bytes 786440 | tf_op jit(solution)/shard_map/while/body/eval_jaxpr/ppermute | solution.py:14
  114.5 10.8 %collective-permute-start = (bf16[128,1,4,128]{3,0,2,1:T(8,128)(2,1)S(1)}, bf16[128,1,4,128]{3,0,2,1:T(8,128)(2,1)S(1)}, u32[]{:S(2)}, u32[]{:S(2)}) collective-permute-start(bf16[128,1,4,128]{3,0,2,1:T(8,128)(2,1)S(1)} %copy.21), channel_id=1, source_target_pairs={{0,8},{8,16},{16,24},{24,32},{32,40},{40,48},{48,56},{56,64},{64,7... | collective-permute-start | bytes 393224 | tf_op jit(solution)/shard_map/while/body/eval_jaxpr/ppermute | solution.py:14
  114.6 10.7 %collective-permute-start.2 = (f32[128,1,4]{0,2,1:T(4,128)S(1)}, f32[128,1,4]{0,2,1:T(4,128)S(1)}, u32[]{:S(2)}, u32[]{:S(2)}) collective-permute-start(f32[128,1,4]{0,2,1:T(4,128)S(1)} %get-tuple-element.431), channel_id=1, source_target_pairs={{0,8},{8,16},{16,24},{24,32},{32,40},{40,48},{48,56},{56,64},{64,7... | collective-permute-start | bytes 6152 | tf_op jit(solution)/shard_map/while/body/eval_jaxpr/ppermute | solution.py:14
  131.6 10.9 %collective-permute-start.1 = (f32[128,1,4,128]{3,0,2,1:T(8,128)S(1)}, f32[128,1,4,128]{3,0,2,1:T(8,128)S(1)}, u32[]{:S(2)}, u32[]{:S(2)}) collective-permute-start(f32[128,1,4,128]{3,0,2,1:T(8,128)S(1)} %fusion.79), channel_id=1, source_target_pairs={{0,8},{8,16},{16,24},{24,32},{32,40},{40,48},{48,56},{56,64},{64,7... | collective-permute-start | bytes 786440 | tf_op jit(solution)/shard_map/while/body/eval_jaxpr/ppermute | solution.py:14
  131.7 10.8 %collective-permute-start = (bf16[128,1,4,128]{3,0,2,1:T(8,128)(2,1)S(1)}, bf16[128,1,4,128]{3,0,2,1:T(8,128)(2,1)S(1)}, u32[]{:S(2)}, u32[]{:S(2)}) collective-permute-start(bf16[128,1,4,128]{3,0,2,1:T(8,128)(2,1)S(1)} %copy.21), channel_id=1, source_target_pairs={{0,8},{8,16},{16,24},{24,32},{32,40},{40,48},{48,56},{56,64},{64,7... | collective-permute-start | bytes 393224 | tf_op jit(solution)/shard_map/while/body/eval_jaxpr/ppermute | solution.py:14
  131.8 10.7 %collective-permute-start.2 = (f32[128,1,4]{0,2,1:T(4,128)S(1)}, f32[128,1,4]{0,2,1:T(4,128)S(1)}, u32[]{:S(2)}, u32[]{:S(2)}) collective-permute-start(f32[128,1,4]{0,2,1:T(4,128)S(1)} %get-tuple-element.431), channel_id=1, source_target_pairs={{0,8},{8,16},{16,24},{24,32},{32,40},{40,48},{48,56},{56,64},{64,7... | collective-permute-start | bytes 6152 | tf_op jit(solution)/shard_map/while/body/eval_jaxpr/ppermute | solution.py:14
  148.7 10.9 %collective-permute-start.1 = (f32[128,1,4,128]{3,0,2,1:T(8,128)S(1)}, f32[128,1,4,128]{3,0,2,1:T(8,128)S(1)}, u32[]{:S(2)}, u32[]{:S(2)}) collective-permute-start(f32[128,1,4,128]{3,0,2,1:T(8,128)S(1)} %fusion.79), channel_id=1, source_target_pairs={{0,8},{8,16},{16,24},{24,32},{32,40},{40,48},{48,56},{56,64},{64,7... | collective-permute-start | bytes 786440 | tf_op jit(solution)/shard_map/while/body/eval_jaxpr/ppermute | solution.py:14
  148.8 10.8 %collective-permute-start = (bf16[128,1,4,128]{3,0,2,1:T(8,128)(2,1)S(1)}, bf16[128,1,4,128]{3,0,2,1:T(8,128)(2,1)S(1)}, u32[]{:S(2)}, u32[]{:S(2)}) collective-permute-start(bf16[128,1,4,128]{3,0,2,1:T(8,128)(2,1)S(1)} %copy.21), channel_id=1, source_target_pairs={{0,8},{8,16},{16,24},{24,32},{32,40},{40,48},{48,56},{56,64},{64,7... | collective-permute-start | bytes 393224 | tf_op jit(solution)/shard_map/while/body/eval_jaxpr/ppermute | solution.py:14
  165.9 10.9 %collective-permute-start.1 = (f32[128,1,4,128]{3,0,2,1:T(8,128)S(1)}, f32[128,1,4,128]{3,0,2,1:T(8,128)S(1)}, u32[]{:S(2)}, u32[]{:S(2)}) collective-permute-start(f32[128,1,4,128]{3,0,2,1:T(8,128)S(1)} %fusion.79), channel_id=1, source_target_pairs={{0,8},{8,16},{16,24},{24,32},{32,40},{40,48},{48,56},{56,64},{64,7... | collective-permute-start | bytes 786440 | tf_op jit(solution)/shard_map/while/body/eval_jaxpr/ppermute | solution.py:14
  165.9 10.8 %collective-permute-start = (bf16[128,1,4,128]{3,0,2,1:T(8,128)(2,1)S(1)}, bf16[128,1,4,128]{3,0,2,1:T(8,128)(2,1)S(1)}, u32[]{:S(2)}, u32[]{:S(2)}) collective-permute-start(bf16[128,1,4,128]{3,0,2,1:T(8,128)(2,1)S(1)} %copy.21), channel_id=1, source_target_pairs={{0,8},{8,16},{16,24},{24,32},{32,40},{40,48},{48,56},{56,64},{64,7... | collective-permute-start | bytes 393224 | tf_op jit(solution)/shard_map/while/body/eval_jaxpr/ppermute | solution.py:14
  183.0 10.9 %collective-permute-start.1 = (f32[128,1,4,128]{3,0,2,1:T(8,128)S(1)}, f32[128,1,4,128]{3,0,2,1:T(8,128)S(1)}, u32[]{:S(2)}, u32[]{:S(2)}) collective-permute-start(f32[128,1,4,128]{3,0,2,1:T(8,128)S(1)} %fusion.79), channel_id=1, source_target_pairs={{0,8},{8,16},{16,24},{24,32},{32,40},{40,48},{48,56},{56,64},{64,7... | collective-permute-start | bytes 786440 | tf_op jit(solution)/shard_map/while/body/eval_jaxpr/ppermute | solution.py:14
  183.1 10.8 %collective-permute-start = (bf16[128,1,4,128]{3,0,2,1:T(8,128)(2,1)S(1)}, bf16[128,1,4,128]{3,0,2,1:T(8,128)(2,1)S(1)}, u32[]{:S(2)}, u32[]{:S(2)}) collective-permute-start(bf16[128,1,4,128]{3,0,2,1:T(8,128)(2,1)S(1)} %copy.21), channel_id=1, source_target_pairs={{0,8},{8,16},{16,24},{24,32},{32,40},{40,48},{48,56},{56,64},{64,7... | collective-permute-start | bytes 393224 | tf_op jit(solution)/shard_map/while/body/eval_jaxpr/ppermute | solution.py:14
  200.1 10.9 %collective-permute-start.1 = (f32[128,1,4,128]{3,0,2,1:T(8,128)S(1)}, f32[128,1,4,128]{3,0,2,1:T(8,128)S(1)}, u32[]{:S(2)}, u32[]{:S(2)}) collective-permute-start(f32[128,1,4,128]{3,0,2,1:T(8,128)S(1)} %fusion.79), channel_id=1, source_target_pairs={{0,8},{8,16},{16,24},{24,32},{32,40},{40,48},{48,56},{56,64},{64,7... | collective-permute-start | bytes 786440 | tf_op jit(solution)/shard_map/while/body/eval_jaxpr/ppermute | solution.py:14
  200.2 10.8 %collective-permute-start = (bf16[128,1,4,128]{3,0,2,1:T(8,128)(2,1)S(1)}, bf16[128,1,4,128]{3,0,2,1:T(8,128)(2,1)S(1)}, u32[]{:S(2)}, u32[]{:S(2)}) collective-permute-start(bf16[128,1,4,128]{3,0,2,1:T(8,128)(2,1)S(1)} %copy.21), channel_id=1, source_target_pairs={{0,8},{8,16},{16,24},{24,32},{32,40},{40,48},{48,56},{56,64},{64,7... | collective-permute-start | bytes 393224 | tf_op jit(solution)/shard_map/while/body/eval_jaxpr/ppermute | solution.py:14
  217.3 10.9 %collective-permute-start.1 = (f32[128,1,4,128]{3,0,2,1:T(8,128)S(1)}, f32[128,1,4,128]{3,0,2,1:T(8,128)S(1)}, u32[]{:S(2)}, u32[]{:S(2)}) collective-permute-start(f32[128,1,4,128]{3,0,2,1:T(8,128)S(1)} %fusion.79), channel_id=1, source_target_pairs={{0,8},{8,16},{16,24},{24,32},{32,40},{40,48},{48,56},{56,64},{64,7... | collective-permute-start | bytes 786440 | tf_op jit(solution)/shard_map/while/body/eval_jaxpr/ppermute | solution.py:14
  217.4 10.8 %collective-permute-start = (bf16[128,1,4,128]{3,0,2,1:T(8,128)(2,1)S(1)}, bf16[128,1,4,128]{3,0,2,1:T(8,128)(2,1)S(1)}, u32[]{:S(2)}, u32[]{:S(2)}) collective-permute-start(bf16[128,1,4,128]{3,0,2,1:T(8,128)(2,1)S(1)} %copy.21), channel_id=1, source_target_pairs={{0,8},{8,16},{16,24},{24,32},{32,40},{40,48},{48,56},{56,64},{64,7... | collective-permute-start | bytes 393224 | tf_op jit(solution)/shard_map/while/body/eval_jaxpr/ppermute | solution.py:14
  234.4 10.9 %collective-permute-start.1 = (f32[128,1,4,128]{3,0,2,1:T(8,128)S(1)}, f32[128,1,4,128]{3,0,2,1:T(8,128)S(1)}, u32[]{:S(2)}, u32[]{:S(2)}) collective-permute-start(f32[128,1,4,128]{3,0,2,1:T(8,128)S(1)} %fusion.79), channel_id=1, source_target_pairs={{0,8},{8,16},{16,24},{24,32},{32,40},{40,48},{48,56},{56,64},{64,7... | collective-permute-start | bytes 786440 | tf_op jit(solution)/shard_map/while/body/eval_jaxpr/ppermute | solution.py:14
  234.5 10.8 %collective-permute-start = (bf16[128,1,4,128]{3,0,2,1:T(8,128)(2,1)S(1)}, bf16[128,1,4,128]{3,0,2,1:T(8,128)(2,1)S(1)}, u32[]{:S(2)}, u32[]{:S(2)}) collective-permute-start(bf16[128,1,4,128]{3,0,2,1:T(8,128)(2,1)S(1)} %copy.21), channel_id=1, source_target_pairs={{0,8},{8,16},{16,24},{24,32},{32,40},{40,48},{48,56},{56,64},{64,7... | collective-permute-start | bytes 393224 | tf_op jit(solution)/shard_map/while/body/eval_jaxpr/ppermute | solution.py:14
  251.5 10.9 %collective-permute-start.1 = (f32[128,1,4,128]{3,0,2,1:T(8,128)S(1)}, f32[128,1,4,128]{3,0,2,1:T(8,128)S(1)}, u32[]{:S(2)}, u32[]{:S(2)}) collective-permute-start(f32[128,1,4,128]{3,0,2,1:T(8,128)S(1)} %fusion.79), channel_id=1, source_target_pairs={{0,8},{8,16},{16,24},{24,32},{32,40},{40,48},{48,56},{56,64},{64,7... | collective-permute-start | bytes 786440 | tf_op jit(solution)/shard_map/while/body/eval_jaxpr/ppermute | solution.py:14
  251.6 10.8 %collective-permute-start = (bf16[128,1,4,128]{3,0,2,1:T(8,128)(2,1)S(1)}, bf16[128,1,4,128]{3,0,2,1:T(8,128)(2,1)S(1)}, u32[]{:S(2)}, u32[]{:S(2)}) collective-permute-start(bf16[128,1,4,128]{3,0,2,1:T(8,128)(2,1)S(1)} %copy.21), channel_id=1, source_target_pairs={{0,8},{8,16},{16,24},{24,32},{32,40},{40,48},{48,56},{56,64},{64,7... | collective-permute-start | bytes 393224 | tf_op jit(solution)/shard_map/while/body/eval_jaxpr/ppermute | solution.py:14
  281.6 140.3 %all-gather.3.cloned.1.call-start = ((), (), s32[]{:S(2)}) async-start(), calls=%async_computation.1 | async-start | bytes 15597568 | tf_op jit(solution)/shard_map/all_gather | solution.py:114
  282.2 210.0 %all-gather.5.cloned.1.call-start = ((), (), s32[]{:S(2)}) async-start(), calls=%async_computation.2 | async-start | bytes 15597568 | tf_op jit(solution)/shard_map/all_gather | solution.py:119
  (52 other events, 491.8 us)
Sparse Core Ops, SparseCore 0:
  281.7 138.4 all-reduce.1
Sparse Core Ops, SparseCore 1:
  284.5 106.7 all-gather.2
  393.6 98.5 all-gather.4
where the time goes:
time: 510 us; the launch traced here: 508 us
  waiting for transfers between devices  275 us (54%)
  starting transfers between devices  93.1 us (18%)
  matrix products  72.5 us (14%)
  other arithmetic  34.6 us (7%)
  between operations  16.4 us (3%)
  local copies, waits for them, and re-layouts  15.1 us (3%)
    psum x1, waiting for transfers between devices, body(): summed = lax.psum(projected.astype(jnp.bfloat16), 'tp').astype(jnp.float32)  137 us
    ppermute x62, starting transfers between devices, shifted(): return lax.ppermute(value, axis, pairs)  92.9 us
    ppermute x62, waiting for transfers between devices, shifted(): return lax.ppermute(value, axis, pairs)  73.8 us
    all_gather x1, waiting for transfers between devices, body(): lax.all_gather(up_weight, 'ctx', axis=0, tiled=True)  62.6 us
    dot_general x16, matrix products, block_partial(): jnp.einsum('qhgd,khd->hqgk', query_block, key_heads, preferred_element_ty...  31.9 us
    dot_general x16, matrix products, block_partial(): jnp.einsum('hqgk,khd->qhgd', weights.astype(jnp.bfloat16), value_heads, p...  20.6 us
    reduce_sum x16, other arithmetic, block_partial(): block_total = jnp.sum(weights, axis=-1)  18.1 us
    le x16, other arithmetic, block_partial(): key_places[None, None, None, :] <= query_places[None, :, None, None]  14.5 us
  transfers between devices with their start and end apart: 65, of which 19 were waited for; matrix products, arithmetic and copies ran while one was open for 2% of the time, Pallas kernels for 0%

commit v1 on v0

v1 whole, which is shorter than its diff:
```python
import functools
import math

import jax
import jax.numpy as jnp
from jax import lax
from jax.experimental import pallas as pl
from jax.experimental.pallas import tpu as pltpu
from jax.sharding import PartitionSpec as P

HD = 128
NT = (((1,), (1,)), ((), ()))
NN = (((1,), (0,)), ((), ()))
MESH = pl.DeviceIdType.MESH
LOW = -1e30
BASE = math.log2(math.e) / math.sqrt(HD)
F32 = jnp.float32
BF16 = jnp.bfloat16
KT = 1024
CHUNKS = 7
CW = 256
EARLY = 2


def hop(r):
    low = r % 4
    return ((low * (low + 1)) // 2) % 4


def kernel(
    q_hbm,
    k_hbm,
    v_hbm,
    exps_ref,
    qp_ref,
    kp_hbm,
    resid_hbm,
    ow_hbm,
    gain_ref,
    gate_hbm,
    up_hbm,
    out_ref,
    q_all,
    kbuf,
    vbuf,
    vt,
    kpraw,
    kposb,
    sa,
    sb,
    ma,
    mb,
    acc_u,
    acc_s,
    cvec,
    usend,
    ssend,
    urecv,
    srecv,
    ow,
    resid,
    rs_send,
    rs_recv,
    sq_send,
    sq_recv,
    gsend,
    gbuf,
    wbuf,
    xsend,
    xrecv,
    pown,
    q_ss,
    q_rs,
    kv_ss,
    kv_rs,
    loc_s,
    ow_s,
    wl_s,
    u_ss,
    u_rs,
    st_ss,
    st_rs,
    d_ss,
    d_rs,
    f_ss,
    f_rs,
    r_ss,
    r_rs,
    p_ss,
    p_rs,
    sq_ss,
    sq_rs,
    g_ss,
    g_rs,
    x_ss,
    x_rs,
):
    c = lax.axis_index("ctx")
    t = lax.axis_index("tp")
    core = c % 2
    z = (c // 2) % 4
    xh = c // 8

    def ctx_at(dx, dz, dc=0):
        return ((xh + dx) % 2) * 8 + ((z + dz + 4) % 4) * 2 + (core + dc) % 2

    partner = ctx_at(0, 0, 1)
    across = ctx_at(1, 0)
    up_z = ctx_at(0, 1)
    down_z = ctx_at(0, 3)

    def remote(src, dst, ss, rs, **dev):
        return pltpu.make_async_remote_copy(
            src_ref=src, dst_ref=dst, send_sem=ss, recv_sem=rs, device_id=dev, device_id_type=MESH
        )

    lq = pltpu.make_async_copy(q_hbm, q_all.at[0], loc_s.at[0])
    lk = pltpu.make_async_copy(k_hbm, kbuf.at[1], loc_s.at[1])
    lv = pltpu.make_async_copy(v_hbm, vbuf.at[1], loc_s.at[2])
    lp = pltpu.make_async_copy(kp_hbm, kpraw.at[1], loc_s.at[3])
    for cp in (lq, lk, lv, lp):
        cp.start()

    barrier = pltpu.get_barrier_semaphore()
    peers = 0
    for r in range(1, 8):
        pl.semaphore_signal(
            barrier, inc=1, device_id={"ctx": ctx_at(r // 4, r % 4), "tp": t}, device_id_type=MESH
        )
        pl.semaphore_signal(
            barrier, inc=1, device_id={"ctx": c, "tp": (t + r) % 8}, device_id_type=MESH
        )
        pl.semaphore_signal(
            barrier, inc=1, device_id={"ctx": across, "tp": (t + r) % 8}, device_id_type=MESH
        )
        peers += 3
    pl.semaphore_signal(barrier, inc=1, device_id={"ctx": partner, "tp": t}, device_id_type=MESH)
    pl.semaphore_wait(barrier, peers + 1)

    kv = [
        remote(k_hbm, kbuf.at[0], kv_ss.at[0], kv_rs.at[0], ctx=partner, tp=t),
        remote(v_hbm, vbuf.at[0], kv_ss.at[1], kv_rs.at[1], ctx=partner, tp=t),
        remote(kp_hbm, kpraw.at[0], kv_ss.at[2], kv_rs.at[2], ctx=partner, tp=t),
    ]

    def q_copy(r):
        return remote(
            q_hbm, q_all.at[r], q_ss.at[r], q_rs.at[r], ctx=ctx_at(r // 4, 4 - hop(r)), tp=t
        )

    kv[2].start()
    for r in (1, 2, 3, 4):
        q_copy(r).start()
    kv[0].start()
    kv[1].start()

    def q_forward(r):
        return remote(q_all.at[r], q_all.at[r + 4], q_ss.at[r + 4], q_rs.at[r + 4], ctx=across, tp=t)

    own_rows = pl.multiple_of(core * 1024 + z * 256, 256)

    def own_weight(j, which):
        src = (gate_hbm, up_hbm)[which]
        return pltpu.make_async_copy(
            src.at[:, pl.ds(j * CW, CW)],
            wbuf.at[j, pl.ds(own_rows, 256), pl.ds(which * CW, CW)],
            wl_s.at[2 * j + which],
        )

    for j in range(CHUNKS):
        own_weight(j, 0).start()
        own_weight(j, 1).start()
    lres = pltpu.make_async_copy(
        resid_hbm.at[:, pl.ds(pl.multiple_of(t * 512, 512), 512)], resid, loc_s.at[4]
    )
    lres.start()

    def ow_copy(s):
        return pltpu.make_async_copy(ow_hbm.at[:, pl.ds(s * 512, 512)], ow.at[s], ow_s.at[s])

    for s in range(8):
        ow_copy(s).start()

    def block(zz):
        return pl.multiple_of(core * 1024 + ((zz + 4) % 4) * 256, 256)

    def direct(j, way):
        rows = pl.ds(own_rows, 256)
        return remote(
            wbuf.at[j, rows],
            wbuf.at[j, rows],
            d_ss.at[way, j],
            d_rs.at[way, j],
            ctx=(up_z, down_z)[way],
            tp=t,
        )

    def direct_both(j):
        direct(j, 0).start()
        direct(j, 1).start()

    def direct_arrival(j, way):
        rows = pl.ds(block(z - 1 if way == 0 else z + 1), 256)
        return remote(
            wbuf.at[j, rows], wbuf.at[j, rows], d_ss.at[way, j], d_rs.at[way, j], ctx=up_z, tp=t
        )

    def forward(j, way):
        at = wbuf.at[j, pl.ds(block(z - 1 if way == 0 else z + 1), 256), pl.ds(way * CW, CW)]
        return remote(at, at, f_ss.at[way, j], f_rs.at[way, j], ctx=(up_z, down_z)[way], tp=t)

    def forward_arrival(j, way):
        at = wbuf.at[j, pl.ds(block(z + 2), 256), pl.ds(way * CW, CW)]
        return remote(at, at, f_ss.at[way, j], f_rs.at[way, j], ctx=up_z, tp=t)

    def pass_on(j):
        for way in (0, 1):
            direct_arrival(j, way).wait_recv()
        for way in (0, 1):
            forward(j, way).start()

    def relay(j):
        at = wbuf.at[j, pl.ds(pl.multiple_of(core * 1024, 1024), 1024)]
        return remote(at, at, r_ss.at[j], r_rs.at[j], ctx=partner, tp=t)

    def relay_arrival(j):
        at = wbuf.at[j, pl.ds(pl.multiple_of((1 - core) * 1024, 1024), 1024)]
        return remote(at, at, r_ss.at[j], r_rs.at[j], ctx=partner, tp=t)

    def hand_over(j):
        for way in (0, 1):
            forward_arrival(j, way).wait_recv()
        relay(j).start()

    def prepare(half):
        def turn(a, _):
            rows = pl.ds(pl.multiple_of(a * 128, 128), 128)
            vt[half, :, rows] = jnp.transpose(vbuf[half, rows, :].astype(F32)).astype(BF16)
            places = jnp.broadcast_to(kpraw[half, pl.ds(a, 1), :].astype(F32), (128, 128))
            kposb[half, rows, :] = jnp.transpose(places)
            return 0

        lax.fori_loop(0, 16, turn, 0)

    cvec[...] = jnp.exp2(jnp.broadcast_to(exps_ref[0:1, :], (8, 128)).astype(F32)) * BASE
    acc_u[...] = jnp.zeros_like(acc_u)
    acc_s[...] = jnp.zeros_like(acc_s)
    for cp in (lq, lk, lv, lp):
        cp.wait()
    prepare(1)

    def qk(i, j, buf, mref):
        r = ((i + 1) // 2) % 8
        half = (i + 1) % 2
        owner = ctx_at(r // 4, hop(r))
        qpos = qp_ref[pl.ds(owner, 1), :].astype(F32)
        qc = jnp.concatenate([q_all[r, :, h * HD : (h + 1) * HD] for h in range(4)], axis=0)
        s = lax.dot_general(
            kbuf[half, j * KT : (j + 1) * KT], qc, NT, preferred_element_type=F32
        )
        visible = kposb[half, j * KT : (j + 1) * KT] <= qpos
        s = jnp.concatenate(
            [jnp.where(visible, s[:, h * HD : (h + 1) * HD], LOW) for h in range(4)], axis=1
        )
        buf[...] = s
        mref[...] = jnp.max(s, axis=0, keepdims=True)

    def pv(i, j, buf, mref, state):
        half = (i + 1) % 2
        factor = cvec[0:1, 0:1]
        top = jnp.maximum(state[0], mref[...])
        p = jnp.exp2((buf[...] - top) * factor)
        total = jnp.sum(p, axis=0, keepdims=True)
        out = lax.dot_general(
            vt[half, :, j * KT : (j + 1) * KT], p.astype(BF16), NN, preferred_element_type=F32
        )
        keep = jnp.exp2((state[0] - top) * factor)
        return (top, state[1] * keep + total, state[2] * keep + out)

    def u_copy(r):
        return remote(
            usend.at[r], urecv.at[r], u_ss.at[r], u_rs.at[r], ctx=ctx_at(r // 4, hop(r)), tp=t
        )

    def s_copy(r):
        return remote(
            ssend.at[r], srecv.at[r], st_ss.at[r], st_rs.at[r], ctx=ctx_at(r // 4, hop(r)), tp=t
        )

    qk(0, 0, sa, ma)

    def step(i, _):
        odd = i % 2
        r = ((i + 1) // 2) % 8
        r_next = ((i + 2) // 2) % 8

        @pl.when(i == 0)
        def _():
            for cp in kv:
                cp.wait_recv()
            prepare(0)

        @pl.when((odd == 0) & (i < 14))
        def _():
            q_copy(r_next).wait_recv()

        @pl.when((odd == 0) & (i < 6))
        def _():
            q_forward(r_next).start()

        for n in range(EARLY):

            @pl.when(i == 5 + 5 * n)
            def _(n=n):
                own_weight(n, 0).wait()
                own_weight(n, 1).wait()
                direct_both(n)

        before = jnp.where(odd == 1, LOW, acc_s[0:1, :])
        before = jnp.where(i == 0, LOW, before)
        state = (before, acc_s[1:2, :], acc_u[...])
        qk(i, 1, sb, mb)
        state = pv(i, 0, sa, ma, state)
        qk(i + 1, 0, sa, ma)
        state = pv(i, 1, sb, mb, state)
        acc_s[0:1, :] = state[0]
        acc_s[1:2, :] = state[1]
        acc_u[...] = state[2]

        @pl.when(odd == 0)
        def _():
            usend[r] = acc_u[...].astype(BF16)
            ssend[r] = acc_s[...]

        @pl.when((odd == 0) & (i > 0))
        def _():
            s_copy(r).start()
            u_copy(r).start()

        return 0

    lax.fori_loop(0, 16, step, 0)

    for j in range(EARLY, CHUNKS):
        own_weight(j, 0).wait()
        own_weight(j, 1).wait()
    direct_both(2)
    pass_on(0)
    direct_both(3)
    pass_on(1)
    for j in range(4, CHUNKS):
        direct_both(j)

    for r in range(1, 8):
        s_copy(r).wait_recv()
    tops = [acc_s[0:1, :], ssend[0, 0:1, :]] + [srecv[r, 0:1, :] for r in range(1, 8)]
    sums = [acc_s[1:2, :], ssend[0, 1:2, :]] + [srecv[r, 1:2, :] for r in range(1, 8)]
    top = functools.reduce(jnp.maximum, tops)
    factor = cvec[0:1, 0:1]
    shares = [jnp.exp2((m - top) * factor) for m in tops]
    total = functools.reduce(jnp.add, [w * l for w, l in zip(shares, sums)])
    merged = acc_u[...] * shares[0] + usend[0].astype(F32) * shares[1]
    for r in range(1, 8):
        u_copy(r).wait_recv()
        merged = merged + urecv[r].astype(F32) * shares[r + 1]
    value_factor = jnp.exp2(jnp.broadcast_to(exps_ref[1:2, :], (8, 128)).astype(F32))[0:1, 0:1]
    merged = merged * (value_factor / total)
    attention = jnp.concatenate(
        [jnp.transpose(merged[:, h * HD : (h + 1) * HD]) for h in range(4)], axis=1
    ).astype(BF16)

    for s in range(8):
        ow_copy(s).wait()

    def p_copy(k):
        return remote(
            rs_send.at[k], rs_recv.at[k], p_ss.at[k], p_rs.at[k], ctx=c, tp=(t + k) % 8
        )

    def sq_copy(k):
        return remote(
            sq_send, sq_recv.at[k], sq_ss.at[k], sq_rs.at[k], ctx=c, tp=(t + k) % 8
        )

    for k in (4, 5, 3, 2, 6, 7, 1):
        part = lax.dot_general(
            attention, ow[(t + k) % 8], NN, preferred_element_type=F32
        )
        rs_send[k] = part.astype(BF16)
        p_copy(k).start()
    stream = lax.dot_general(attention, ow[t], NN, preferred_element_type=F32)
    lres.wait()
    stream = stream + resid[...].astype(F32)
    for k in range(1, 8):
        p_copy(k).wait_recv()
        stream = stream + rs_recv[k].astype(F32)

    squares = lax.dot_general(
        jnp.ones((8, 512), F32),
        stream * stream,
        NT,
        preferred_element_type=F32,
        precision=lax.Precision.HIGHEST,
    )
    sq_send[...] = squares
    for k in range(1, 8):
        sq_copy(k).start()

    gain = gain_ref[0:1, pl.ds(pl.multiple_of(t * 512, 512), 512)].astype(F32)
    scaled = (stream * gain).astype(BF16)
    gsend[0] = scaled[:, :256]
    gsend[1] = scaled[:, 256:]
    to_half = t // 4
    lane = pl.ds(pl.multiple_of((t % 4) * 256, 256), 256)
    to_ctx = to_half * 8 + z * 2 + core
    side = (xh + to_half) % 2

    def g_copy(k):
        return remote(
            gsend,
            gbuf.at[:, side, :, lane],
            g_ss.at[k],
            g_rs.at[side * 4 + t % 4],
            ctx=to_ctx,
            tp=(t + k) % 8,
        )

    for k in (4, 3, 5, 2, 6, 1, 7):
        g_copy(k).start()

    @pl.when(side == 1)
    def _():
        g_copy(0).start()

    @pl.when(side == 0)
    def _():
        gbuf[0, 0, :, lane] = gsend[0]
        gbuf[1, 0, :, lane] = gsend[1]

    pass_on(2)
    pass_on(3)
    hand_over(0)
    hand_over(1)

    squares = sq_send[...]
    for k in range(1, 8):
        sq_copy(k).wait_recv()
        squares = squares + sq_recv[k]
    scale_row = lax.rsqrt(squares[0:1, :] * (1.0 / 4096.0) + 1e-05)
    scale = jnp.transpose(jnp.broadcast_to(scale_row, (128, 128)))[:, 0:1]

    def g_arrival(slot):
        at = gbuf.at[:, slot // 4, :, pl.ds((slot % 4) * 256, 256)]
        return remote(at, at, g_ss.at[0], g_rs.at[slot], ctx=across, tp=t)

    for slot in range(8):
        if slot < 4:

            @pl.when((to_half != xh) | (t % 4 != slot))
            def _(slot=slot):
                g_arrival(slot).wait_recv()
        else:
            g_arrival(slot).wait_recv()

    def x_copy(j):
        return remote(xsend.at[j], xrecv.at[j], x_ss.at[j], x_rs.at[j], ctx=across, tp=t)

    def finish(j):
        x_copy(j).wait_recv()
        both = (pown[j] + xrecv[j].astype(F32)) * scale
        gate = both[:, :CW]
        up = both[:, CW:]
        out_ref[:, pl.ds(pl.multiple_of(j * CW, CW), CW)] = (gate / (1.0 + jnp.exp(-gate)) * up).astype(BF16)

    def chunk(j, _):
        @pl.when(j < CHUNKS - 4)
        def _():
            pass_on(j + 4)

        relay_arrival(j).wait_recv()

        def half_product(which):
            return lax.dot_general(
                gbuf[0, which], wbuf[j, 0:1024, :], NN, preferred_element_type=F32
            ) + lax.dot_general(
                gbuf[1, which], wbuf[j, 1024:2048, :], NN, preferred_element_type=F32
            )

        xsend[j] = half_product(1).astype(BF16)
        x_copy(j).start()

        @pl.when(j < CHUNKS - 2)
        def _():
            hand_over(j + 2)

        pown[j] = half_product(0)

        @pl.when(j >= 2)
        def _():
            finish(j - 2)

        return 0

    lax.fori_loop(0, CHUNKS, chunk, 0)
    finish(CHUNKS - 2)
    finish(CHUNKS - 1)

    for cp in kv:
        cp.wait_send()
    for r in (1, 2, 3, 4):
        q_copy(r).wait_send()
    for r in (1, 2, 3):
        q_forward(r).wait_send()
    for r in range(1, 8):
        u_copy(r).wait_send()
        s_copy(r).wait_send()
        p_copy(r).wait_send()
        sq_copy(r).wait_send()
        g_copy(r).wait_send()

    @pl.when(side == 1)
    def _():
        g_copy(0).wait_send()

    for j in range(CHUNKS):
        for way in (0, 1):
            direct(j, way).wait_send()
            forward(j, way).wait_send()
        relay(j).wait_send()
        x_copy(j).wait_send()


def body(
    queries,
    key_cache,
    value_cache,
    scale_exps,
    query_pos,
    key_pos,
    resid,
    out_weight,
    norm_gain,
    gate_weight,
    up_weight,
):
    vmem = pl.BlockSpec(memory_space=pltpu.VMEM)
    hbm = pl.BlockSpec(memory_space=pl.ANY)
    V = pltpu.VMEM
    dma = pltpu.SemaphoreType.DMA
    return pl.pallas_call(
        kernel,
        out_shape=jax.ShapeDtypeStruct((128, 1792), BF16),
        in_specs=[hbm, hbm, hbm, vmem, vmem, hbm, hbm, hbm, vmem, hbm, hbm],
        out_specs=vmem,
        scratch_shapes=[
            V((8, 128, 512), BF16),
            V((2, 2048, 128), BF16),
            V((2, 2048, 128), BF16),
            V((2, 128, 2048), BF16),
            V((2, 16, 128), jnp.int32),
            V((2, 2048, 128), F32),
            V((KT, 512), F32),
            V((KT, 512), F32),
            V((1, 512), F32),
            V((1, 512), F32),
            V((128, 512), F32),
            V((8, 512), F32),
            V((8, 128), F32),
            V((8, 128, 512), BF16),
            V((8, 8, 512), F32),
            V((8, 128, 512), BF16),
            V((8, 8, 512), F32),
            V((8, 512, 512), BF16),
            V((128, 512), BF16),
            V((8, 128, 512), BF16),
            V((8, 128, 512), BF16),
            V((8, 128), F32),
            V((8, 8, 128), F32),
            V((2, 128, 256), BF16),
            V((2, 2, 128, 1024), BF16),
            V((CHUNKS, 2048, 2 * CW), BF16),
            V((CHUNKS, 128, 2 * CW), BF16),
            V((CHUNKS, 128, 2 * CW), BF16),
            V((CHUNKS, 128, 2 * CW), F32),
            dma((8,)),
            dma((8,)),
            dma((3,)),
            dma((3,)),
            dma((5,)),
            dma((8,)),
            dma((2 * CHUNKS,)),
            dma((8,)),
            dma((8,)),
            dma((8,)),
            dma((8,)),
            dma((2, CHUNKS)),
            dma((2, CHUNKS)),
            dma((2, CHUNKS)),
            dma((2, CHUNKS)),
            dma((CHUNKS,)),
            dma((CHUNKS,)),
            dma((8,)),
            dma((8,)),
            dma((8,)),
            dma((8,)),
            dma((8,)),
            dma((8,)),
            dma((CHUNKS,)),
            dma((CHUNKS,)),
        ],
        compiler_params=pltpu.CompilerParams(
            collective_id=0, has_side_effects=True, vmem_limit_bytes=60 * 2**20
        ),
        cost_estimate=pl.CostEstimate(
            flops=18_000_000_000, bytes_accessed=16_000_000, transcendentals=17_000_000
        ),
    )(
        queries,
        key_cache,
        value_cache,
        scale_exps,
        query_pos.reshape(16, 128),
        key_pos.reshape(16, 128),
        resid,
        out_weight,
        norm_gain.reshape(1, 4096),
        gate_weight,
        up_weight,
    )


def solution(mesh):
    placed = (
        P("ctx", "tp"),
        P("ctx", "tp"),
        P("ctx", "tp"),
        P(None, "tp"),
        P(),
        P("ctx"),
        P("ctx", None),
        P("tp", None),
        P(),
        P("ctx", "tp"),
        P("ctx", "tp"),
    )
    return jax.shard_map(
        body, mesh=mesh, in_specs=placed, out_specs=P("ctx", "tp"), check_vma=False
    )
```

time: 510 us -> 135 us (0.26)
  the two profiles are of different devices: /device:TPU:1 before, /device:TPU:30 now
where the time goes in v1:
time: 135 us
  Pallas kernels  130 us (96%)
  local copies, waits for them, and re-layouts  4.44 us (3%)
    pallas_call x1, Pallas kernels, body(): pl.pallas_call(kernel, out_shape=jax.ShapeDtypeStruct((128, 1792), BF16),...  130 us
    unnamed x2, local copies, waits for them, and re-layouts  3.13 us

profile of v1, /device:TPU:30, one launch (start us, length us, event | category | flops | bytes accessed | tf_op | source)
XLA Modules:
  0.0 134.8 jit_solution(13073628263724840763)
XLA Ops:
  0.0 1.3 copy.12.exps_ref
  1.3 1.3 reshape.11.gain_ref
  2.6 130.3 %shard_map.109 = bf16[128,1792]{1,0:T(8,128)(2,1)} custom-call(bf16[128,512]{1,0:T(8,128)(2,1)} %q_hbm.1, bf16[2048,128]{1,0:T(8,128)(2,1)} %k_hbm.1, bf16[2048,128]{1,0:T(8,128)(2,1)} %v_hbm.1, s32[2,1]{1,0:T(2,128)} %copy.12.exps_ref, s32[16,128]{1,0:T(8,128)} %bitcast.2, s32[16,128]{1,0:T(8,128)} %bitcast.3, bf16[128,4096]{1,0:T(8,128)(2,1)} %resid_hbm.1, ...), custom_call_target="tpu_custom_call" | custom-call | flops 17999998976 | bytes 16000000 | tf_op jit(solution)/shard_map/pallas_call | solution.py:550
  132.9 1.8 %copy.14 = bf16[128,1792]{1,0:T(8,128)(2,1)} copy(bf16[128,1792]{1,0:T(8,128)(2,1)} %shard_map.109) | data formatting | bytes 917504

commit v2 on v1

--- a/solution.py
+++ b/solution.py
@@ -19,12 +19,18 @@
 KT = 1024
 CHUNKS = 7
 CW = 256
-EARLY = 2
+EARLY = 3
 
 
 def hop(r):
     low = r % 4
     return ((low * (low + 1)) // 2) % 4
+
+
+def turn_owner(n):
+    n = n % 8
+    late = n // 4
+    return late * (4 + (n + 1) % 4) + (1 - late) * n
 
 
 def kernel(
@@ -36,7 +42,7 @@
     kp_hbm,
     resid_hbm,
     ow_hbm,
-    gain_ref,
+    gain_hbm,
     gate_hbm,
     up_hbm,
     out_ref,
@@ -57,18 +63,23 @@
     ssend,
     urecv,
     srecv,
+    uhalf,
+    shalf,
     ow,
     resid,
+    gain_buf,
     rs_send,
     rs_recv,
     sq_send,
     sq_recv,
+    sq_other,
     gsend,
     gbuf,
     wbuf,
     xsend,
     xrecv,
     pown,
+    scale,
     q_ss,
     q_rs,
     kv_ss,
@@ -80,6 +91,8 @@
     u_rs,
     st_ss,
     st_rs,
+    uh_rs,
+    sh_rs,
     d_ss,
     d_rs,
     f_ss,
@@ -170,15 +183,22 @@
     for j in range(CHUNKS):
         own_weight(j, 0).start()
         own_weight(j, 1).start()
-    lres = pltpu.make_async_copy(
-        resid_hbm.at[:, pl.ds(pl.multiple_of(t * 512, 512), 512)], resid, loc_s.at[4]
+    def feature(half):
+        return pl.ds(pl.multiple_of(half * 2048 + t * 256, 256), 256)
+
+    lres = pltpu.make_async_copy(resid_hbm.at[:, feature(xh)], resid.at[0], loc_s.at[4])
+    lgain = pltpu.make_async_copy(gain_hbm.at[feature(xh)], gain_buf, loc_s.at[5])
+    rres = remote(
+        resid_hbm.at[:, feature(1 - xh)], resid.at[1], kv_ss.at[3], kv_rs.at[3], ctx=across, tp=t
     )
+    rres.start()
     lres.start()
+    lgain.start()
 
     def ow_copy(s):
-        return pltpu.make_async_copy(ow_hbm.at[:, pl.ds(s * 512, 512)], ow.at[s], ow_s.at[s])
-
-    for s in range(8):
+        return pltpu.make_async_copy(ow_hbm.at[:, pl.ds(s * 256, 256)], ow.at[s], ow_s.at[s])
+
+    for s in range(16):
         ow_copy(s).start()
 
     def block(zz):
@@ -240,9 +260,9 @@
             kposb[half, rows, :] = jnp.transpose(places)
             return 0
 
-        lax.fori_loop(0, 16, turn, 0)
-
-    cvec[...] = jnp.exp2(jnp.broadcast_to(exps_ref[0:1, :], (8, 128)).astype(F32)) * BASE
+        lax.fori_loop(0, 16, turn, 0, unroll=4)
+
+    cvec[...] = jnp.exp2(jnp.broadcast_to(exps_ref[0:1, 0:1], (8, 128)).astype(F32)) * BASE
     acc_u[...] = jnp.zeros_like(acc_u)
     acc_s[...] = jnp.zeros_like(acc_s)
     for cp in (lq, lk, lv, lp):
@@ -250,7 +270,7 @@
     prepare(1)
 
     def qk(i, j, buf, mref):
-        r = ((i + 1) // 2) % 8
+        r = turn_owner((i + 1) // 2)
         half = (i + 1) % 2
         owner = ctx_at(r // 4, hop(r))
         qpos = qp_ref[pl.ds(owner, 1), :].astype(F32)
@@ -278,21 +298,36 @@
         return (top, state[1] * keep + total, state[2] * keep + out)
 
     def u_copy(r):
-        return remote(
-            usend.at[r], urecv.at[r], u_ss.at[r], u_rs.at[r], ctx=ctx_at(r // 4, hop(r)), tp=t
-        )
+        return remote(usend.at[r], urecv.at[r], u_ss.at[r], u_rs.at[r], ctx=ctx_at(0, hop(r)), tp=t)
 
     def s_copy(r):
-        return remote(
-            ssend.at[r], srecv.at[r], st_ss.at[r], st_rs.at[r], ctx=ctx_at(r // 4, hop(r)), tp=t
-        )
+        return remote(ssend.at[r], srecv.at[r], st_ss.at[r], st_rs.at[r], ctx=ctx_at(0, hop(r)), tp=t)
+
+    def u_across(r):
+        return remote(usend.at[r], uhalf.at[r - 4], u_ss.at[r], uh_rs.at[r - 4], ctx=across, tp=t)
+
+    def s_across(r):
+        return remote(ssend.at[r], shalf.at[r - 4], st_ss.at[r], sh_rs.at[r - 4], ctx=across, tp=t)
+
+    def combine(r):
+        s_across(r + 4).wait_recv()
+        u_across(r + 4).wait_recv()
+        factor = cvec[0:1, 0:1]
+        mine, theirs = ssend[r, 0:1, :], shalf[r, 0:1, :]
+        top = jnp.maximum(mine, theirs)
+        keep, add = jnp.exp2((mine - top) * factor), jnp.exp2((theirs - top) * factor)
+        ssend[r, 0:1, :] = top
+        ssend[r, 1:2, :] = ssend[r, 1:2, :] * keep + shalf[r, 1:2, :] * add
+        usend[r] = (usend[r].astype(F32) * keep + uhalf[r].astype(F32) * add).astype(BF16)
+        s_copy(r).start()
+        u_copy(r).start()
 
     qk(0, 0, sa, ma)
 
     def step(i, _):
         odd = i % 2
-        r = ((i + 1) // 2) % 8
-        r_next = ((i + 2) // 2) % 8
+        r = turn_owner((i + 1) // 2)
+        r_next = turn_owner((i + 2) // 2)
 
         @pl.when(i == 0)
         def _():
@@ -300,6 +335,12 @@
                 cp.wait_recv()
             prepare(0)
 
+        for n in range(3):
+
+            @pl.when(i == 11 + 2 * n)
+            def _(n=n):
+                combine(n + 1)
+
         @pl.when((odd == 0) & (i < 14))
         def _():
             q_copy(r_next).wait_recv()
@@ -310,7 +351,7 @@
 
         for n in range(EARLY):
 
-            @pl.when(i == 5 + 5 * n)
+            @pl.when(i == 3 * n)
             def _(n=n):
                 own_weight(n, 0).wait()
                 own_weight(n, 1).wait()
@@ -332,168 +373,176 @@
             usend[r] = acc_u[...].astype(BF16)
             ssend[r] = acc_s[...]
 
-        @pl.when((odd == 0) & (i > 0))
-        def _():
-            s_copy(r).start()
-            u_copy(r).start()
+        @pl.when((odd == 0) & (i > 6))
+        def _():
+            s_across(r).start()
+            u_across(r).start()
 
         return 0
 
     lax.fori_loop(0, 16, step, 0)
 
     for j in range(EARLY, CHUNKS):
-        own_weight(j, 0).wait()
-        own_weight(j, 1).wait()
-    direct_both(2)
-    pass_on(0)
-    direct_both(3)
-    pass_on(1)
-    for j in range(4, CHUNKS):
+        for which in (0, 1):
+            own_weight(j, which).wait()
+    for j in range(EARLY, CHUNKS):
         direct_both(j)
-
-    for r in range(1, 8):
+        if j < CHUNKS - 1:
+            pass_on(j - EARLY)
+
+    for r in (1, 2, 3):
         s_copy(r).wait_recv()
-    tops = [acc_s[0:1, :], ssend[0, 0:1, :]] + [srecv[r, 0:1, :] for r in range(1, 8)]
-    sums = [acc_s[1:2, :], ssend[0, 1:2, :]] + [srecv[r, 1:2, :] for r in range(1, 8)]
+    s_across(4).wait_recv()
+    tops = [acc_s[0:1, :], ssend[0, 0:1, :], shalf[0, 0:1, :]] + [srecv[r, 0:1, :] for r in (1, 2, 3)]
+    sums = [acc_s[1:2, :], ssend[0, 1:2, :], shalf[0, 1:2, :]] + [srecv[r, 1:2, :] for r in (1, 2, 3)]
     top = functools.reduce(jnp.maximum, tops)
     factor = cvec[0:1, 0:1]
     shares = [jnp.exp2((m - top) * factor) for m in tops]
     total = functools.reduce(jnp.add, [w * l for w, l in zip(shares, sums)])
     merged = acc_u[...] * shares[0] + usend[0].astype(F32) * shares[1]
-    for r in range(1, 8):
+    u_across(4).wait_recv()
+    merged = merged + uhalf[0].astype(F32) * shares[2]
+    for r in (1, 2, 3):
         u_copy(r).wait_recv()
-        merged = merged + urecv[r].astype(F32) * shares[r + 1]
-    value_factor = jnp.exp2(jnp.broadcast_to(exps_ref[1:2, :], (8, 128)).astype(F32))[0:1, 0:1]
+        merged = merged + urecv[r].astype(F32) * shares[r + 2]
+    value_factor = jnp.exp2(jnp.broadcast_to(exps_ref[0:1, 1:2], (8, 128)).astype(F32))[0:1, 0:1]
     merged = merged * (value_factor / total)
     attention = jnp.concatenate(
         [jnp.transpose(merged[:, h * HD : (h + 1) * HD]) for h in range(4)], axis=1
     ).astype(BF16)
 
-    for s in range(8):
-        ow_copy(s).wait()
-
-    def p_copy(k):
+    for n in range(16):
+        ow_copy(n).wait()
+
+    def p_copy(side, k):
         return remote(
-            rs_send.at[k], rs_recv.at[k], p_ss.at[k], p_rs.at[k], ctx=c, tp=(t + k) % 8
+            rs_send.at[side, k],
+            rs_recv.at[side, k],
+            p_ss.at[side, k],
+            p_rs.at[side, k],
+            ctx=(c, across)[side],
+            tp=(t + k) % 8,
+        )
+
+    def product(side, k):
+        half = (xh, 1 - xh)[side]
+        return lax.dot_general(attention, ow[half * 8 + (t + k) % 8], NN, preferred_element_type=F32)
+
+    for k in (0, 4, 3, 5, 2, 6, 1, 7):
+        rs_send[1, k] = product(1, k).astype(BF16)
+        p_copy(1, k).start()
+    for k in (4, 3, 5, 2, 6, 1, 7):
+        rs_send[0, k] = product(0, k).astype(BF16)
+        p_copy(0, k).start()
+    own = product(0, 0)
+    lres.wait()
+    lgain.wait()
+    rres.wait_recv()
+    gain = jnp.broadcast_to(gain_buf[...].astype(F32).reshape(1, 256), (128, 256))
+
+    def g_copy(side, k):
+        lane = pl.ds(pl.multiple_of((t // 2) * 256, 256), 256)
+        return remote(
+            gsend.at[side],
+            gbuf.at[t % 2, side, :, lane],
+            g_ss.at[side, k],
+            g_rs.at[side, k],
+            ctx=c,
+            tp=(t + k) % 8,
+        )
+
+    def spread(side):
+        stream = resid[side].astype(F32)
+        if side == 0:
+            stream = stream + own
+        for k in range(1 - side, 8):
+            p_copy(side, k).wait_recv()
+            stream = stream + rs_recv[side, k].astype(F32)
+        scaled = (stream * gain).astype(BF16)
+        gsend[side] = scaled
+        for k in (4, 3, 5, 2, 6, 1, 7):
+            g_copy(side, k).start()
+        lane = pl.ds(pl.multiple_of((t // 2) * 256, 256), 256)
+        gbuf[t % 2, side, :, lane] = scaled
+        sq_send[side] = lax.dot_general(
+            jnp.ones((8, 256), F32),
+            stream * stream,
+            NT,
+            preferred_element_type=F32,
+            precision=lax.Precision.HIGHEST,
         )
 
     def sq_copy(k):
-        return remote(
-            sq_send, sq_recv.at[k], sq_ss.at[k], sq_rs.at[k], ctx=c, tp=(t + k) % 8
-        )
-
-    for k in (4, 5, 3, 2, 6, 7, 1):
-        part = lax.dot_general(
-            attention, ow[(t + k) % 8], NN, preferred_element_type=F32
-        )
-        rs_send[k] = part.astype(BF16)
-        p_copy(k).start()
-    stream = lax.dot_general(attention, ow[t], NN, preferred_element_type=F32)
-    lres.wait()
-    stream = stream + resid[...].astype(F32)
-    for k in range(1, 8):
-        p_copy(k).wait_recv()
-        stream = stream + rs_recv[k].astype(F32)
-
-    squares = lax.dot_general(
-        jnp.ones((8, 512), F32),
-        stream * stream,
-        NT,
-        preferred_element_type=F32,
-        precision=lax.Precision.HIGHEST,
-    )
-    sq_send[...] = squares
+        return remote(sq_send, sq_recv.at[k], sq_ss.at[k], sq_rs.at[k], ctx=c, tp=(t + k) % 8)
+
+    def sq_swap():
+        return remote(sq_recv.at[0, 1], sq_other, sq_ss.at[0], sq_rs.at[0], ctx=across, tp=t)
+
+    spread(1)
+    pass_on(3)
+    spread(0)
     for k in range(1, 8):
         sq_copy(k).start()
-
-    gain = gain_ref[0:1, pl.ds(pl.multiple_of(t * 512, 512), 512)].astype(F32)
-    scaled = (stream * gain).astype(BF16)
-    gsend[0] = scaled[:, :256]
-    gsend[1] = scaled[:, 256:]
-    to_half = t // 4
-    lane = pl.ds(pl.multiple_of((t % 4) * 256, 256), 256)
-    to_ctx = to_half * 8 + z * 2 + core
-    side = (xh + to_half) % 2
-
-    def g_copy(k):
-        return remote(
-            gsend,
-            gbuf.at[:, side, :, lane],
-            g_ss.at[k],
-            g_rs.at[side * 4 + t % 4],
-            ctx=to_ctx,
-            tp=(t + k) % 8,
-        )
-
-    for k in (4, 3, 5, 2, 6, 1, 7):
-        g_copy(k).start()
-
-    @pl.when(side == 1)
-    def _():
-        g_copy(0).start()
-
-    @pl.when(side == 0)
-    def _():
-        gbuf[0, 0, :, lane] = gsend[0]
-        gbuf[1, 0, :, lane] = gsend[1]
-
-    pass_on(2)
-    pass_on(3)
+    pass_on(4)
     hand_over(0)
-    hand_over(1)
-
-    squares = sq_send[...]
-    for k in range(1, 8):
-        sq_copy(k).wait_recv()
-        squares = squares + sq_recv[k]
-    scale_row = lax.rsqrt(squares[0:1, :] * (1.0 / 4096.0) + 1e-05)
-    scale = jnp.transpose(jnp.broadcast_to(scale_row, (128, 128)))[:, 0:1]
-
-    def g_arrival(slot):
-        at = gbuf.at[:, slot // 4, :, pl.ds((slot % 4) * 256, 256)]
-        return remote(at, at, g_ss.at[0], g_rs.at[slot], ctx=across, tp=t)
-
-    for slot in range(8):
-        if slot < 4:
-
-            @pl.when((to_half != xh) | (t % 4 != slot))
-            def _(slot=slot):
-                g_arrival(slot).wait_recv()
-        else:
-            g_arrival(slot).wait_recv()
+
+    for side in (1, 0):
+        squares = sq_send[side]
+        for k in range(1, 8):
+            if side == 1:
+                sq_copy(k).wait_recv()
+            squares = squares + sq_recv[k, side]
+        sq_recv[0, side] = squares
+        if side == 1:
+            sq_swap().start()
+
+    def g_arrival(side, k):
+        at = gbuf.at[0, side, :, pl.ds(0, 256)]
+        return remote(at, at, g_ss.at[side, k], g_rs.at[side, k], ctx=across, tp=t)
 
     def x_copy(j):
         return remote(xsend.at[j], xrecv.at[j], x_ss.at[j], x_rs.at[j], ctx=across, tp=t)
 
     def finish(j):
         x_copy(j).wait_recv()
-        both = (pown[j] + xrecv[j].astype(F32)) * scale
+        both = (pown[j] + xrecv[j].astype(F32)) * scale[:, 0:1]
         gate = both[:, :CW]
         up = both[:, CW:]
         out_ref[:, pl.ds(pl.multiple_of(j * CW, CW), CW)] = (gate / (1.0 + jnp.exp(-gate)) * up).astype(BF16)
 
+    def half_product(j, side):
+        return lax.dot_general(
+            gbuf[0, side], wbuf[j, 0:1024, :], NN, preferred_element_type=F32
+        ) + lax.dot_general(
+            gbuf[1, side], wbuf[j, 1024:2048, :], NN, preferred_element_type=F32
+        )
+
+    for k in range(1, 8):
+        g_arrival(1, k).wait_recv()
+
     def chunk(j, _):
-        @pl.when(j < CHUNKS - 4)
-        def _():
-            pass_on(j + 4)
+        @pl.when(j < 2)
+        def _():
+            pass_on(j + 5)
+
+        @pl.when(j < CHUNKS - 1)
+        def _():
+            hand_over(j + 1)
 
         relay_arrival(j).wait_recv()
-
-        def half_product(which):
-            return lax.dot_general(
-                gbuf[0, which], wbuf[j, 0:1024, :], NN, preferred_element_type=F32
-            ) + lax.dot_general(
-                gbuf[1, which], wbuf[j, 1024:2048, :], NN, preferred_element_type=F32
-            )
-
-        xsend[j] = half_product(1).astype(BF16)
+        xsend[j] = half_product(j, 1).astype(BF16)
         x_copy(j).start()
 
-        @pl.when(j < CHUNKS - 2)
-        def _():
-            hand_over(j + 2)
-
-        pown[j] = half_product(0)
+        @pl.when(j == 0)
+        def _():
+            for k in range(1, 8):
+                g_arrival(0, k).wait_recv()
+            sq_swap().wait_recv()
+            squares = sq_recv[0, 0, 0:1, :] + sq_other[0:1, :]
+            scale_row = lax.rsqrt(squares * (1.0 / 4096.0) + 1e-05)
+            scale[...] = jnp.transpose(jnp.broadcast_to(scale_row, (128, 128)))
+
+        pown[j] = half_product(j, 0)
 
         @pl.when(j >= 2)
         def _():
@@ -507,21 +556,24 @@
 
     for cp in kv:
         cp.wait_send()
+    rres.wait_send()
     for r in (1, 2, 3, 4):
         q_copy(r).wait_send()
     for r in (1, 2, 3):
         q_forward(r).wait_send()
-    for r in range(1, 8):
         u_copy(r).wait_send()
         s_copy(r).wait_send()
-        p_copy(r).wait_send()
-        sq_copy(r).wait_send()
-        g_copy(r).wait_send()
-
-    @pl.when(side == 1)
-    def _():
-        g_copy(0).wait_send()
-
+    for r in (4, 5, 6, 7):
+        u_across(r).wait_send()
+        s_across(r).wait_send()
+    for k in range(8):
+        p_copy(1, k).wait_send()
+        if k:
+            p_copy(0, k).wait_send()
+            g_copy(1, k).wait_send()
+            g_copy(0, k).wait_send()
+            sq_copy(k).wait_send()
+    sq_swap().wait_send()
     for j in range(CHUNKS):
         for way in (0, 1):
             direct(j, way).wait_send()
@@ -550,7 +602,7 @@
     return pl.pallas_call(
         kernel,
         out_shape=jax.ShapeDtypeStruct((128, 1792), BF16),
-        in_specs=[hbm, hbm, hbm, vmem, vmem, hbm, hbm, hbm, vmem, hbm, hbm],
+        in_specs=[hbm, hbm, hbm, vmem, vmem, hbm, hbm, hbm, hbm, hbm, hbm],
         out_specs=vmem,
         scratch_shapes=[
             V((8, 128, 512), BF16),
@@ -568,43 +620,50 @@
             V((8, 128), F32),
             V((8, 128, 512), BF16),
             V((8, 8, 512), F32),
-            V((8, 128, 512), BF16),
-            V((8, 8, 512), F32),
-            V((8, 512, 512), BF16),
-            V((128, 512), BF16),
-            V((8, 128, 512), BF16),
-            V((8, 128, 512), BF16),
+            V((4, 128, 512), BF16),
+            V((4, 8, 512), F32),
+            V((4, 128, 512), BF16),
+            V((4, 8, 512), F32),
+            V((16, 512, 256), BF16),
+            V((2, 128, 256), BF16),
+            V((256,), BF16),
+            V((2, 8, 128, 256), BF16),
+            V((2, 8, 128, 256), BF16),
+            V((2, 8, 128), F32),
+            V((8, 2, 8, 128), F32),
             V((8, 128), F32),
-            V((8, 8, 128), F32),
             V((2, 128, 256), BF16),
             V((2, 2, 128, 1024), BF16),
             V((CHUNKS, 2048, 2 * CW), BF16),
             V((CHUNKS, 128, 2 * CW), BF16),
             V((CHUNKS, 128, 2 * CW), BF16),
             V((CHUNKS, 128, 2 * CW), F32),
+            V((128, 128), F32),
             dma((8,)),
             dma((8,)),
-            dma((3,)),
-            dma((3,)),
-            dma((5,)),
-            dma((8,)),
+            dma((4,)),
+            dma((4,)),
+            dma((6,)),
+            dma((16,)),
             dma((2 * CHUNKS,)),
             dma((8,)),
+            dma((4,)),
             dma((8,)),
-            dma((8,)),
-            dma((8,)),
+            dma((4,)),
+            dma((4,)),
+            dma((4,)),
             dma((2, CHUNKS)),
             dma((2, CHUNKS)),
             dma((2, CHUNKS)),
             dma((2, CHUNKS)),
             dma((CHUNKS,)),
             dma((CHUNKS,)),
+            dma((2, 8)),
+            dma((2, 8)),
             dma((8,)),
             dma((8,)),
-            dma((8,)),
-            dma((8,)),
-            dma((8,)),
-            dma((8,)),
+            dma((2, 8)),
+            dma((2, 8)),
             dma((CHUNKS,)),
             dma((CHUNKS,)),
         ],
@@ -618,12 +677,12 @@
         queries,
         key_cache,
         value_cache,
-        scale_exps,
+        scale_exps.T,
         query_pos.reshape(16, 128),
         key_pos.reshape(16, 128),
         resid,
         out_weight,
-        norm_gain.reshape(1, 4096),
+        norm_gain,
         gate_weight,
         up_weight,
     )

time: 135 us -> 104 us (0.77)
  the two profiles are of different devices: /device:TPU:30 before, /device:TPU:1 now
where the time goes in v2:
time: 104 us; the launch traced here: 103 us
  Pallas kernels  102 us (98%)
  local copies, waits for them, and re-layouts  1.82 us (2%)
    pallas_call x1, Pallas kernels, body(): pl.pallas_call(kernel, out_shape=jax.ShapeDtypeStruct((128, 1792), BF16),...  102 us

profile of v2, /device:TPU:1, one launch (start us, length us, event | category | flops | bytes accessed | tf_op | source)
XLA Modules:
  0.0 103.5 jit_solution(4652147252503997738)
XLA Ops:
  0.0 101.7 %shard_map.109 = bf16[128,1792]{1,0:T(8,128)(2,1)} custom-call(bf16[128,512]{1,0:T(8,128)(2,1)} %q_hbm.1, bf16[2048,128]{1,0:T(8,128)(2,1)} %k_hbm.1, bf16[2048,128]{1,0:T(8,128)(2,1)} %v_hbm.1, s32[1,2]{1,0:T(1,128)} %bitcast.5, s32[16,128]{1,0:T(8,128)} %bitcast.3, s32[16,128]{1,0:T(8,128)} %bitcast.4, bf16[128,4096]{1,0:T(8,128)(2,1)} %resid_hbm.1, ...), custom_call_target="tpu_custom_call" | custom-call | flops 17999998976 | bytes 16000000 | tf_op jit(solution)/shard_map/pallas_call | solution.py:602
  101.7 1.8 %copy.13 = bf16[128,1792]{1,0:T(8,128)(2,1)} copy(bf16[128,1792]{1,0:T(8,128)(2,1)} %shard_map.109) | data formatting | bytes 917504

commit v3 on v2

--- a/solution.py
+++ b/solution.py
@@ -19,7 +19,7 @@
 KT = 1024
 CHUNKS = 7
 CW = 256
-EARLY = 3
+EARLY = 4
 
 
 def hop(r):
@@ -29,8 +29,8 @@
 
 def turn_owner(n):
     n = n % 8
-    late = n // 4
-    return late * (4 + (n + 1) % 4) + (1 - late) * n
+    late, m = n // 4, n % 4
+    return late * (7 - 2 * (m % 2) - m // 2) + (1 - late) * n
 
 
 def kernel(
@@ -158,7 +158,7 @@
 
     def q_copy(r):
         return remote(
-            q_hbm, q_all.at[r], q_ss.at[r], q_rs.at[r], ctx=ctx_at(r // 4, 4 - hop(r)), tp=t
+            q_hbm, q_all.at[r], q_ss, q_rs.at[r], ctx=ctx_at(r // 4, 4 - hop(r)), tp=t
         )
 
     kv[2].start()
@@ -168,7 +168,7 @@
     kv[1].start()
 
     def q_forward(r):
-        return remote(q_all.at[r], q_all.at[r + 4], q_ss.at[r + 4], q_rs.at[r + 4], ctx=across, tp=t)
+        return remote(q_all.at[r], q_all.at[r + 4], q_ss, q_rs.at[r + 4], ctx=across, tp=t)
 
     own_rows = pl.multiple_of(core * 1024 + z * 256, 256)
 
@@ -177,7 +177,7 @@
         return pltpu.make_async_copy(
             src.at[:, pl.ds(j * CW, CW)],
             wbuf.at[j, pl.ds(own_rows, 256), pl.ds(which * CW, CW)],
-            wl_s.at[2 * j + which],
+            wl_s,
         )
 
     for j in range(CHUNKS):
@@ -196,7 +196,7 @@
     lgain.start()
 
     def ow_copy(s):
-        return pltpu.make_async_copy(ow_hbm.at[:, pl.ds(s * 256, 256)], ow.at[s], ow_s.at[s])
+        return pltpu.make_async_copy(ow_hbm.at[:, pl.ds(s * 256, 256)], ow.at[s], ow_s)
 
     for s in range(16):
         ow_copy(s).start()
@@ -209,8 +209,8 @@
         return remote(
             wbuf.at[j, rows],
             wbuf.at[j, rows],
-            d_ss.at[way, j],
-            d_rs.at[way, j],
+            d_ss,
+            d_rs.at[j],
             ctx=(up_z, down_z)[way],
             tp=t,
         )
@@ -219,38 +219,30 @@
         direct(j, 0).start()
         direct(j, 1).start()
 
-    def direct_arrival(j, way):
-        rows = pl.ds(block(z - 1 if way == 0 else z + 1), 256)
-        return remote(
-            wbuf.at[j, rows], wbuf.at[j, rows], d_ss.at[way, j], d_rs.at[way, j], ctx=up_z, tp=t
-        )
+    def arrived(ref, sem):
+        remote(ref, ref, d_ss, sem, ctx=partner, tp=t).wait_recv()
+
+    def left(ref, sem):
+        remote(ref, ref, sem, d_rs.at[0], ctx=partner, tp=t).wait_send()
 
     def forward(j, way):
         at = wbuf.at[j, pl.ds(block(z - 1 if way == 0 else z + 1), 256), pl.ds(way * CW, CW)]
-        return remote(at, at, f_ss.at[way, j], f_rs.at[way, j], ctx=(up_z, down_z)[way], tp=t)
-
-    def forward_arrival(j, way):
-        at = wbuf.at[j, pl.ds(block(z + 2), 256), pl.ds(way * CW, CW)]
-        return remote(at, at, f_ss.at[way, j], f_rs.at[way, j], ctx=up_z, tp=t)
+        return remote(at, at, f_ss, f_rs.at[j], ctx=(up_z, down_z)[way], tp=t)
+
+    def relay(j, dz):
+        at = wbuf.at[j, pl.ds(block(z + dz), 256)]
+        return remote(at, at, r_ss, r_rs.at[j], ctx=partner, tp=t)
 
     def pass_on(j):
-        for way in (0, 1):
-            direct_arrival(j, way).wait_recv()
+        arrived(wbuf.at[j, 0:512], d_rs.at[j])
         for way in (0, 1):
             forward(j, way).start()
-
-    def relay(j):
-        at = wbuf.at[j, pl.ds(pl.multiple_of(core * 1024, 1024), 1024)]
-        return remote(at, at, r_ss.at[j], r_rs.at[j], ctx=partner, tp=t)
-
-    def relay_arrival(j):
-        at = wbuf.at[j, pl.ds(pl.multiple_of((1 - core) * 1024, 1024), 1024)]
-        return remote(at, at, r_ss.at[j], r_rs.at[j], ctx=partner, tp=t)
+        for dz in (0, 1, 3):
+            relay(j, dz).start()
 
     def hand_over(j):
-        for way in (0, 1):
-            forward_arrival(j, way).wait_recv()
-        relay(j).start()
+        arrived(wbuf.at[j, 0:256], f_rs.at[j])
+        relay(j, 2).start()
 
     def prepare(half):
         def turn(a, _):
@@ -298,16 +290,16 @@
         return (top, state[1] * keep + total, state[2] * keep + out)
 
     def u_copy(r):
-        return remote(usend.at[r], urecv.at[r], u_ss.at[r], u_rs.at[r], ctx=ctx_at(0, hop(r)), tp=t)
+        return remote(usend.at[r], urecv.at[r], u_ss, u_rs, ctx=ctx_at(0, hop(r)), tp=t)
 
     def s_copy(r):
-        return remote(ssend.at[r], srecv.at[r], st_ss.at[r], st_rs.at[r], ctx=ctx_at(0, hop(r)), tp=t)
+        return remote(ssend.at[r], srecv.at[r], st_ss, st_rs, ctx=ctx_at(0, hop(r)), tp=t)
 
     def u_across(r):
-        return remote(usend.at[r], uhalf.at[r - 4], u_ss.at[r], uh_rs.at[r - 4], ctx=across, tp=t)
+        return remote(usend.at[r], uhalf.at[r - 4], u_ss, uh_rs.at[r - 4], ctx=across, tp=t)
 
     def s_across(r):
-        return remote(ssend.at[r], shalf.at[r - 4], st_ss.at[r], sh_rs.at[r - 4], ctx=across, tp=t)
+        return remote(ssend.at[r], shalf.at[r - 4], st_ss, sh_rs.at[r - 4], ctx=across, tp=t)
 
     def combine(r):
         s_across(r + 4).wait_recv()
@@ -329,18 +321,27 @@
         r = turn_owner((i + 1) // 2)
         r_next = turn_owner((i + 2) // 2)
 
+        for n, (at, r_z) in enumerate(((12, 3), (14, 1), (15, 2))):
+
+            @pl.when(i == at)
+            def _(r_z=r_z):
+                combine(r_z)
+
+        for n in range(EARLY):
+
+            @pl.when(i == 3 * n)
+            def _(n=n):
+                if n == 0:
+                    mine = wbuf.at[:, pl.ds(own_rows, 256)]
+                    pltpu.make_async_copy(mine, mine, wl_s).wait()
+                direct_both(n)
+
         @pl.when(i == 0)
         def _():
             for cp in kv:
                 cp.wait_recv()
             prepare(0)
 
-        for n in range(3):
-
-            @pl.when(i == 11 + 2 * n)
-            def _(n=n):
-                combine(n + 1)
-
         @pl.when((odd == 0) & (i < 14))
         def _():
             q_copy(r_next).wait_recv()
@@ -348,14 +349,6 @@
         @pl.when((odd == 0) & (i < 6))
         def _():
             q_forward(r_next).start()
-
-        for n in range(EARLY):
-
-            @pl.when(i == 3 * n)
-            def _(n=n):
-                own_weight(n, 0).wait()
-                own_weight(n, 1).wait()
-                direct_both(n)
 
         before = jnp.where(odd == 1, LOW, acc_s[0:1, :])
         before = jnp.where(i == 0, LOW, before)
@@ -383,15 +376,10 @@
     lax.fori_loop(0, 16, step, 0)
 
     for j in range(EARLY, CHUNKS):
-        for which in (0, 1):
-            own_weight(j, which).wait()
-    for j in range(EARLY, CHUNKS):
         direct_both(j)
-        if j < CHUNKS - 1:
-            pass_on(j - EARLY)
-
-    for r in (1, 2, 3):
-        s_copy(r).wait_recv()
+        pass_on(j - EARLY)
+
+    arrived(srecv.at[1:4], st_rs)
     s_across(4).wait_recv()
     tops = [acc_s[0:1, :], ssend[0, 0:1, :], shalf[0, 0:1, :]] + [srecv[r, 0:1, :] for r in (1, 2, 3)]
     sums = [acc_s[1:2, :], ssend[0, 1:2, :], shalf[0, 1:2, :]] + [srecv[r, 1:2, :] for r in (1, 2, 3)]
@@ -402,8 +390,8 @@
     merged = acc_u[...] * shares[0] + usend[0].astype(F32) * shares[1]
     u_across(4).wait_recv()
     merged = merged + uhalf[0].astype(F32) * shares[2]
+    arrived(urecv.at[1:4], u_rs)
     for r in (1, 2, 3):
-        u_copy(r).wait_recv()
         merged = merged + urecv[r].astype(F32) * shares[r + 2]
     value_factor = jnp.exp2(jnp.broadcast_to(exps_ref[0:1, 1:2], (8, 128)).astype(F32))[0:1, 0:1]
     merged = merged * (value_factor / total)
@@ -411,15 +399,14 @@
         [jnp.transpose(merged[:, h * HD : (h + 1) * HD]) for h in range(4)], axis=1
     ).astype(BF16)
 
-    for n in range(16):
-        ow_copy(n).wait()
+    pltpu.make_async_copy(ow, ow, ow_s).wait()
 
     def p_copy(side, k):
         return remote(
             rs_send.at[side, k],
             rs_recv.at[side, k],
-            p_ss.at[side, k],
-            p_rs.at[side, k],
+            p_ss.at[side],
+            p_rs.at[side],
             ctx=(c, across)[side],
             tp=(t + k) % 8,
         )
@@ -445,8 +432,8 @@
         return remote(
             gsend.at[side],
             gbuf.at[t % 2, side, :, lane],
-            g_ss.at[side, k],
-            g_rs.at[side, k],
+            g_ss.at[side],
+            g_rs.at[side],
             ctx=c,
             tp=(t + k) % 8,
         )
@@ -455,8 +442,8 @@
         stream = resid[side].astype(F32)
         if side == 0:
             stream = stream + own
+        arrived(rs_recv.at[side, 1 - side : 8], p_rs.at[side])
         for k in range(1 - side, 8):
-            p_copy(side, k).wait_recv()
             stream = stream + rs_recv[side, k].astype(F32)
         scaled = (stream * gain).astype(BF16)
         gsend[side] = scaled
@@ -473,10 +460,10 @@
         )
 
     def sq_copy(k):
-        return remote(sq_send, sq_recv.at[k], sq_ss.at[k], sq_rs.at[k], ctx=c, tp=(t + k) % 8)
+        return remote(sq_send, sq_recv.at[k], sq_ss.at[0], sq_rs.at[0], ctx=c, tp=(t + k) % 8)
 
     def sq_swap():
-        return remote(sq_recv.at[0, 1], sq_other, sq_ss.at[0], sq_rs.at[0], ctx=across, tp=t)
+        return remote(sq_recv.at[0, 1], sq_other, sq_ss.at[1], sq_rs.at[1], ctx=across, tp=t)
 
     spread(1)
     pass_on(3)
@@ -486,22 +473,20 @@
     pass_on(4)
     hand_over(0)
 
-    for side in (1, 0):
-        squares = sq_send[side]
-        for k in range(1, 8):
-            if side == 1:
-                sq_copy(k).wait_recv()
-            squares = squares + sq_recv[k, side]
-        sq_recv[0, side] = squares
-        if side == 1:
-            sq_swap().start()
-
-    def g_arrival(side, k):
-        at = gbuf.at[0, side, :, pl.ds(0, 256)]
-        return remote(at, at, g_ss.at[side, k], g_rs.at[side, k], ctx=across, tp=t)
+    def swap_squares():
+        arrived(sq_recv.at[1:8], sq_rs.at[0])
+        for side in (1, 0):
+            squares = sq_send[side]
+            for k in range(1, 8):
+                squares = squares + sq_recv[k, side]
+            sq_recv[0, side] = squares
+        sq_swap().start()
+
+    def g_arrival(side):
+        arrived(rs_recv.at[0, 1:8], g_rs.at[side])
 
     def x_copy(j):
-        return remote(xsend.at[j], xrecv.at[j], x_ss.at[j], x_rs.at[j], ctx=across, tp=t)
+        return remote(xsend.at[j], xrecv.at[j], x_ss, x_rs.at[j], ctx=across, tp=t)
 
     def finish(j):
         x_copy(j).wait_recv()
@@ -517,8 +502,23 @@
             gbuf[1, side], wbuf[j, 1024:2048, :], NN, preferred_element_type=F32
         )
 
-    for k in range(1, 8):
-        g_arrival(1, k).wait_recv()
+    def drain():
+        for cp in kv:
+            cp.wait_send()
+        rres.wait_send()
+        left(q_all.at[1:8], q_ss)
+        left(usend.at[1:8], u_ss)
+        left(ssend.at[1:8], st_ss)
+        left(rs_send.at[1], p_ss.at[1])
+        for ref in (p_ss.at[0], g_ss.at[0], g_ss.at[1]):
+            left(rs_send.at[0, 1:8], ref)
+        left(sq_recv.at[1:8], sq_ss.at[0])
+        sq_swap().wait_send()
+        left(wbuf.at[:, 0:512], d_ss)
+        left(wbuf.at[:, 0:256], f_ss)
+        left(wbuf.at[:, 0:1024], r_ss)
+
+    g_arrival(1)
 
     def chunk(j, _):
         @pl.when(j < 2)
@@ -529,57 +529,40 @@
         def _():
             hand_over(j + 1)
 
-        relay_arrival(j).wait_recv()
+        arrived(wbuf.at[j, 0:1024], r_rs.at[j])
         xsend[j] = half_product(j, 1).astype(BF16)
         x_copy(j).start()
 
-        @pl.when(j == 0)
-        def _():
-            for k in range(1, 8):
-                g_arrival(0, k).wait_recv()
+        @pl.when(j == 2)
+        def _():
+            g_arrival(0)
+            swap_squares()
+
+        @pl.when(j >= 2)
+        def _():
+            pown[j - 2] = half_product(j - 2, 0)
+
+        @pl.when(j == 4)
+        def _():
             sq_swap().wait_recv()
             squares = sq_recv[0, 0, 0:1, :] + sq_other[0:1, :]
             scale_row = lax.rsqrt(squares * (1.0 / 4096.0) + 1e-05)
             scale[...] = jnp.transpose(jnp.broadcast_to(scale_row, (128, 128)))
 
-        pown[j] = half_product(j, 0)
-
-        @pl.when(j >= 2)
-        def _():
-            finish(j - 2)
+        @pl.when(j >= 4)
+        def _():
+            finish(j - 4)
 
         return 0
 
     lax.fori_loop(0, CHUNKS, chunk, 0)
-    finish(CHUNKS - 2)
-    finish(CHUNKS - 1)
-
-    for cp in kv:
-        cp.wait_send()
-    rres.wait_send()
-    for r in (1, 2, 3, 4):
-        q_copy(r).wait_send()
-    for r in (1, 2, 3):
-        q_forward(r).wait_send()
-        u_copy(r).wait_send()
-        s_copy(r).wait_send()
-    for r in (4, 5, 6, 7):
-        u_across(r).wait_send()
-        s_across(r).wait_send()
-    for k in range(8):
-        p_copy(1, k).wait_send()
-        if k:
-            p_copy(0, k).wait_send()
-            g_copy(1, k).wait_send()
-            g_copy(0, k).wait_send()
-            sq_copy(k).wait_send()
-    sq_swap().wait_send()
-    for j in range(CHUNKS):
-        for way in (0, 1):
-            direct(j, way).wait_send()
-            forward(j, way).wait_send()
-        relay(j).wait_send()
-        x_copy(j).wait_send()
+
+    drain()
+    for j in range(CHUNKS - 4, CHUNKS):
+        if j >= CHUNKS - 2:
+            pown[j] = half_product(j, 0)
+        finish(j)
+    left(xsend, x_ss)
 
 
 def body(
@@ -601,7 +584,7 @@
     dma = pltpu.SemaphoreType.DMA
     return pl.pallas_call(
         kernel,
-        out_shape=jax.ShapeDtypeStruct((128, 1792), BF16),
+        out_shape=pltpu.VMEM((128, 1792), BF16),
         in_specs=[hbm, hbm, hbm, vmem, vmem, hbm, hbm, hbm, hbm, hbm, hbm],
         out_specs=vmem,
         scratch_shapes=[
@@ -639,32 +622,32 @@
             V((CHUNKS, 128, 2 * CW), BF16),
             V((CHUNKS, 128, 2 * CW), F32),
             V((128, 128), F32),
-            dma((8,)),
+            dma,
             dma((8,)),
             dma((4,)),
             dma((4,)),
             dma((6,)),
-            dma((16,)),
-            dma((2 * CHUNKS,)),
-            dma((8,)),
-            dma((4,)),
-            dma((8,)),
+            dma,
+            dma,
+            dma,
+            dma,
+            dma,
+            dma,
             dma((4,)),
             dma((4,)),
-            dma((4,)),
-            dma((2, CHUNKS)),
-            dma((2, CHUNKS)),
-            dma((2, CHUNKS)),
-            dma((2, CHUNKS)),
+            dma,
             dma((CHUNKS,)),
+            dma,
             dma((CHUNKS,)),
-            dma((2, 8)),
-            dma((2, 8)),
-            dma((8,)),
-            dma((8,)),
-            dma((2, 8)),
-            dma((2, 8)),
+            dma,
             dma((CHUNKS,)),
+            dma((2,)),
+            dma((2,)),
+            dma((2,)),
+            dma((2,)),
+            dma((2,)),
+            dma((2,)),
+            dma,
             dma((CHUNKS,)),
         ],
         compiler_params=pltpu.CompilerParams(

time: 104 us -> 94.9 us (0.913)
  Pallas kernels: 102 us -> 94 us
  local copies, waits for them, and re-layouts: 1.82 us -> 0.77 us
    pallas_call x1, Pallas kernels: 102 us -> 94 us  [body(): pl.pallas_call(kernel, out_shape=pltpu.VMEM((128, 1792), BF16), in_specs=...]
    unnamed x1, local copies, waits for them, and re-layouts: 1.82 us -> 0.77 us
where the time goes in v3:
time: 94.9 us; the launch traced here: 94.8 us
  Pallas kernels  94 us (99%)
    pallas_call x1, Pallas kernels, body(): pl.pallas_call(kernel, out_shape=pltpu.VMEM((128, 1792), BF16), in_specs=...  94 us

profile of v3, /device:TPU:1, one launch (start us, length us, event | category | flops | bytes accessed | tf_op | source)
XLA Modules:
  0.0 94.8 jit_solution(18307995825410807706)
XLA Ops:
  0.0 94.0 %shard_map.109 = bf16[128,1792]{1,0:T(8,128)(2,1)S(1)} custom-call(bf16[128,512]{1,0:T(8,128)(2,1)} %q_hbm.1, bf16[2048,128]{1,0:T(8,128)(2,1)} %k_hbm.1, bf16[2048,128]{1,0:T(8,128)(2,1)} %v_hbm.1, s32[1,2]{1,0:T(1,128)} %bitcast.5, s32[16,128]{1,0:T(8,128)} %bitcast.3, s32[16,128]{1,0:T(8,128)} %bitcast.4, bf16[128,4096]{1,0:T(8,128)(2,1)} %resid_hbm.1, ...), custom_call_target="tpu_custom_call" | custom-call | flops 17999998976 | bytes 16000000 | tf_op jit(solution)/shard_map/pallas_call | solution.py:585
  94.0 0.8 copy.13

commit v4 on v3

--- a/solution.py
+++ b/solution.py
@@ -17,9 +17,9 @@
 F32 = jnp.float32
 BF16 = jnp.bfloat16
 KT = 1024
-CHUNKS = 7
-CW = 256
-EARLY = 4
+CHUNKS = 14
+CW = 128
+LAG = 7
 
 
 def hop(r):
@@ -29,8 +29,7 @@
 
 def turn_owner(n):
     n = n % 8
-    late, m = n // 4, n % 4
-    return late * (7 - 2 * (m % 2) - m // 2) + (1 - late) * n
+    return n + 3 * ((n + 6) // 8) - 4 * ((n + 3) // 8) - 2 * ((n + 2) // 8) - 2 * (n // 7)
 
 
 def kernel(
@@ -67,13 +66,23 @@
     shalf,
     ow,
     resid,
+    resid_own,
     gain_buf,
+    gain_wide,
     rs_send,
     rs_recv,
-    sq_send,
+    ws_send,
+    ws_recv,
+    swap_send,
+    swap_recv,
+    own,
+    far_squares,
+    own_squares,
     sq_recv,
+    oq_recv,
     sq_other,
     gsend,
+    gsend_wide,
     gbuf,
     wbuf,
     xsend,
@@ -101,6 +110,10 @@
     r_rs,
     p_ss,
     p_rs,
+    w_ss,
+    w_rs,
+    sw_ss,
+    sw_rs,
     sq_ss,
     sq_rs,
     g_ss,
@@ -134,42 +147,6 @@
     for cp in (lq, lk, lv, lp):
         cp.start()
 
-    barrier = pltpu.get_barrier_semaphore()
-    peers = 0
-    for r in range(1, 8):
-        pl.semaphore_signal(
-            barrier, inc=1, device_id={"ctx": ctx_at(r // 4, r % 4), "tp": t}, device_id_type=MESH
-        )
-        pl.semaphore_signal(
-            barrier, inc=1, device_id={"ctx": c, "tp": (t + r) % 8}, device_id_type=MESH
-        )
-        pl.semaphore_signal(
-            barrier, inc=1, device_id={"ctx": across, "tp": (t + r) % 8}, device_id_type=MESH
-        )
-        peers += 3
-    pl.semaphore_signal(barrier, inc=1, device_id={"ctx": partner, "tp": t}, device_id_type=MESH)
-    pl.semaphore_wait(barrier, peers + 1)
-
-    kv = [
-        remote(k_hbm, kbuf.at[0], kv_ss.at[0], kv_rs.at[0], ctx=partner, tp=t),
-        remote(v_hbm, vbuf.at[0], kv_ss.at[1], kv_rs.at[1], ctx=partner, tp=t),
-        remote(kp_hbm, kpraw.at[0], kv_ss.at[2], kv_rs.at[2], ctx=partner, tp=t),
-    ]
-
-    def q_copy(r):
-        return remote(
-            q_hbm, q_all.at[r], q_ss, q_rs.at[r], ctx=ctx_at(r // 4, 4 - hop(r)), tp=t
-        )
-
-    kv[2].start()
-    for r in (1, 2, 3, 4):
-        q_copy(r).start()
-    kv[0].start()
-    kv[1].start()
-
-    def q_forward(r):
-        return remote(q_all.at[r], q_all.at[r + 4], q_ss, q_rs.at[r + 4], ctx=across, tp=t)
-
     own_rows = pl.multiple_of(core * 1024 + z * 256, 256)
 
     def own_weight(j, which):
@@ -183,23 +160,71 @@
     for j in range(CHUNKS):
         own_weight(j, 0).start()
         own_weight(j, 1).start()
-    def feature(half):
-        return pl.ds(pl.multiple_of(half * 2048 + t * 256, 256), 256)
-
-    lres = pltpu.make_async_copy(resid_hbm.at[:, feature(xh)], resid.at[0], loc_s.at[4])
-    lgain = pltpu.make_async_copy(gain_hbm.at[feature(xh)], gain_buf, loc_s.at[5])
+
+    barrier = pltpu.get_barrier_semaphore()
+    peers = 0
+    for r in range(1, 8):
+        pl.semaphore_signal(
+            barrier, inc=1, device_id={"ctx": ctx_at(r // 4, r % 4), "tp": t}, device_id_type=MESH
+        )
+        pl.semaphore_signal(
+            barrier, inc=1, device_id={"ctx": c, "tp": (t + r) % 8}, device_id_type=MESH
+        )
+        pl.semaphore_signal(
+            barrier, inc=1, device_id={"ctx": across, "tp": (t + r) % 8}, device_id_type=MESH
+        )
+        peers += 3
+    pl.semaphore_signal(barrier, inc=1, device_id={"ctx": partner, "tp": t}, device_id_type=MESH)
+    pl.semaphore_wait(barrier, peers + 1)
+
+    kv = [
+        remote(k_hbm, kbuf.at[0], kv_ss.at[0], kv_rs.at[0], ctx=partner, tp=t),
+        remote(v_hbm, vbuf.at[0], kv_ss.at[1], kv_rs.at[1], ctx=partner, tp=t),
+        remote(kp_hbm, kpraw.at[0], kv_ss.at[2], kv_rs.at[2], ctx=partner, tp=t),
+    ]
+
+    def q_copy(r):
+        return remote(
+            q_hbm, q_all.at[r], q_ss, q_rs.at[r], ctx=ctx_at(r // 4, 4 - hop(r)), tp=t
+        )
+
+    kv[2].start()
+    for r in (1, 2, 4):
+        q_copy(r).start()
+    kv[0].start()
+    kv[1].start()
+
+    def q_pass(r):
+        rows = pl.ds(pl.multiple_of(64 * (r - 1), 64), 64)
+        return remote(
+            q_all.at[r, rows], q_all.at[3, rows], q_ss, q_rs.at[3], ctx=ctx_at(0, 5 - 2 * r), tp=t
+        )
+
+    def q_forward(r):
+        return remote(q_all.at[r], q_all.at[r + 4], q_ss, q_rs.at[r + 4], ctx=across, tp=t)
+
+    y = t // 2
+    piece = pl.ds(pl.multiple_of(xh * 2048 + t * 256, 256), 256)
+    far_piece = pl.ds(pl.multiple_of((1 - xh) * 2048 + t * 256, 256), 256)
+    wide = pl.ds(pl.multiple_of(xh * 2048 + y * 512, 512), 512)
+
+    lres = pltpu.make_async_copy(resid_hbm.at[:, wide], resid_own, loc_s.at[4])
+    lgain = pltpu.make_async_copy(gain_hbm.at[piece], gain_buf, loc_s.at[5])
+    lwide = pltpu.make_async_copy(gain_hbm.at[wide], gain_wide, loc_s.at[6])
     rres = remote(
-        resid_hbm.at[:, feature(1 - xh)], resid.at[1], kv_ss.at[3], kv_rs.at[3], ctx=across, tp=t
+        resid_hbm.at[:, far_piece], resid, kv_ss.at[3], kv_rs.at[3], ctx=across, tp=t
     )
-    rres.start()
-    lres.start()
-    lgain.start()
 
     def ow_copy(s):
         return pltpu.make_async_copy(ow_hbm.at[:, pl.ds(s * 256, 256)], ow.at[s], ow_s)
 
-    for s in range(16):
-        ow_copy(s).start()
+    def later_loads():
+        rres.start()
+        lres.start()
+        lgain.start()
+        lwide.start()
+        for s in range(16):
+            ow_copy(s).start()
 
     def block(zz):
         return pl.multiple_of(core * 1024 + ((zz + 4) % 4) * 256, 256)
@@ -314,44 +339,62 @@
         s_copy(r).start()
         u_copy(r).start()
 
+    mine = wbuf.at[:, pl.ds(own_rows, 256)]
+    pltpu.make_async_copy(mine, mine, wl_s).wait()
+    direct_both(0)
     qk(0, 0, sa, ma)
+    qk(0, 1, sb, mb)
+    state = (jnp.full((1, 512), LOW, F32), jnp.zeros((1, 512), F32), jnp.zeros((128, 512), F32))
+    state = pv(0, 0, sa, ma, state)
+    state = pv(0, 1, sb, mb, state)
+    ssend[0, 0:1, :] = state[0]
+    ssend[0, 1:2, :] = state[1]
+    usend[0] = state[2].astype(BF16)
+    for cp in kv:
+        cp.wait_recv()
+    prepare(0)
+    for r in (1, 2):
+        q_copy(r).wait_recv()
+        q_pass(r).start()
+        q_forward(r).start()
+    direct_both(1)
+    qk(1, 0, sa, ma)
 
     def step(i, _):
         odd = i % 2
         r = turn_owner((i + 1) // 2)
         r_next = turn_owner((i + 2) // 2)
 
-        for n, (at, r_z) in enumerate(((12, 3), (14, 1), (15, 2))):
-
-            @pl.when(i == at)
-            def _(r_z=r_z):
-                combine(r_z)
-
-        for n in range(EARLY):
-
-            @pl.when(i == 3 * n)
-            def _(n=n):
-                if n == 0:
-                    mine = wbuf.at[:, pl.ds(own_rows, 256)]
-                    pltpu.make_async_copy(mine, mine, wl_s).wait()
-                direct_both(n)
-
-        @pl.when(i == 0)
-        def _():
-            for cp in kv:
-                cp.wait_recv()
-            prepare(0)
-
-        @pl.when((odd == 0) & (i < 14))
+        @pl.when((odd == 1) & (i > 10))
+        def _():
+            m = (i - 11) // 2
+            combine(1 + 2 * m - 3 * (m // 2))
+
+            @pl.when(i == 15)
+            def _():
+                pass_on(3)
+                direct_both(6)
+
+        @pl.when((odd == 0) & (i < 9))
+        def _():
+            direct_both(i // 2 + 1)
+
+        @pl.when((i == 4) | (i == 6) | (i == 9))
+        def _():
+            pass_on(i // 3 - 1)
+
+        pl.when(i == 7)(later_loads)
+
+        @pl.when(i == 3)
+        def _():
+            q_copy(3).wait_recv()
+            q_forward(3).start()
+
+        @pl.when((odd == 0) & (i < 10))
         def _():
             q_copy(r_next).wait_recv()
 
-        @pl.when((odd == 0) & (i < 6))
-        def _():
-            q_forward(r_next).start()
-
         before = jnp.where(odd == 1, LOW, acc_s[0:1, :])
-        before = jnp.where(i == 0, LOW, before)
         state = (before, acc_s[1:2, :], acc_u[...])
         qk(i, 1, sb, mb)
         state = pv(i, 0, sa, ma, state)
@@ -366,18 +409,20 @@
             usend[r] = acc_u[...].astype(BF16)
             ssend[r] = acc_s[...]
 
-        @pl.when((odd == 0) & (i > 6))
-        def _():
-            s_across(r).start()
-            u_across(r).start()
+            @pl.when((i > 2) & (i < 12))
+            def _():
+                s_across(r).start()
+                u_across(r).start()
 
         return 0
 
-    lax.fori_loop(0, 16, step, 0)
-
-    for j in range(EARLY, CHUNKS):
+    lax.fori_loop(1, 16, step, 0)
+
+    pass_on(4)
+    direct_both(7)
+    pass_on(5)
+    for j in (8, 9, 10):
         direct_both(j)
-        pass_on(j - EARLY)
 
     arrived(srecv.at[1:4], st_rs)
     s_across(4).wait_recv()
@@ -401,89 +446,143 @@
 
     pltpu.make_async_copy(ow, ow, ow_s).wait()
 
-    def p_copy(side, k):
-        return remote(
-            rs_send.at[side, k],
-            rs_recv.at[side, k],
-            p_ss.at[side],
-            p_rs.at[side],
-            ctx=(c, across)[side],
-            tp=(t + k) % 8,
-        )
-
-    def product(side, k):
-        half = (xh, 1 - xh)[side]
-        return lax.dot_general(attention, ow[half * 8 + (t + k) % 8], NN, preferred_element_type=F32)
+    def peer(k):
+        return ((y + k) % 4) * 2 + t % 2
+
+    neighbour = y * 2 + 1 - t % 2
+
+    def p_copy(k):
+        return remote(rs_send.at[k], rs_recv.at[k], p_ss, p_rs, ctx=across, tp=(t + k) % 8)
+
+    def w_copy(k):
+        return remote(ws_send.at[k], ws_recv.at[k], w_ss, w_rs, ctx=c, tp=peer(k))
+
+    def swap_copy():
+        return remote(swap_send, swap_recv, sw_ss, sw_rs, ctx=c, tp=neighbour)
+
+    def product(at):
+        return lax.dot_general(attention, ow[at], NN, preferred_element_type=F32)
 
     for k in (0, 4, 3, 5, 2, 6, 1, 7):
-        rs_send[1, k] = product(1, k).astype(BF16)
-        p_copy(1, k).start()
-    for k in (4, 3, 5, 2, 6, 1, 7):
-        rs_send[0, k] = product(0, k).astype(BF16)
-        p_copy(0, k).start()
-    own = product(0, 0)
+        rs_send[k] = product((1 - xh) * 8 + (t + k) % 8).astype(BF16)
+        p_copy(k).start()
+    for k in (2, 1, 3):
+        at = xh * 8 + ((y + k) % 4) * 2
+        ws_send[k, :, 0:256] = product(at).astype(BF16)
+        ws_send[k, :, 256:512] = product(at + 1).astype(BF16)
+        w_copy(k).start()
+    own[:, 0:256] = product(xh * 8 + y * 2)
+    own[:, 256:512] = product(xh * 8 + y * 2 + 1)
     lres.wait()
     lgain.wait()
+    lwide.wait()
     rres.wait_recv()
-    gain = jnp.broadcast_to(gain_buf[...].astype(F32).reshape(1, 256), (128, 256))
-
-    def g_copy(side, k):
-        lane = pl.ds(pl.multiple_of((t // 2) * 256, 256), 256)
+
+    lane = pl.ds(pl.multiple_of(y * 256, 256), 256)
+
+    def g_cross():
+        at = gbuf.at[t % 2, 1, :, lane]
+        return remote(gsend, at, g_ss.at[2], g_rs.at[2], ctx=c, tp=neighbour)
+
+    def g_copy(k):
+        at = gbuf.at[t % 2, 1, :, lane]
+        return remote(gsend, at, g_ss.at[1], g_rs.at[1], ctx=c, tp=peer(k))
+
+    def g_forward(k):
+        at = gbuf.at[1 - t % 2, 1, :, lane]
+        return remote(at, at, g_ss.at[1], g_rs.at[1], ctx=c, tp=peer(k))
+
+    def gw_copy(k):
         return remote(
-            gsend.at[side],
-            gbuf.at[t % 2, side, :, lane],
-            g_ss.at[side],
-            g_rs.at[side],
-            ctx=c,
-            tp=(t + k) % 8,
-        )
-
-    def spread(side):
-        stream = resid[side].astype(F32)
-        if side == 0:
-            stream = stream + own
-        arrived(rs_recv.at[side, 1 - side : 8], p_rs.at[side])
-        for k in range(1 - side, 8):
-            stream = stream + rs_recv[side, k].astype(F32)
-        scaled = (stream * gain).astype(BF16)
-        gsend[side] = scaled
-        for k in (4, 3, 5, 2, 6, 1, 7):
-            g_copy(side, k).start()
-        lane = pl.ds(pl.multiple_of((t // 2) * 256, 256), 256)
-        gbuf[t % 2, side, :, lane] = scaled
-        sq_send[side] = lax.dot_general(
-            jnp.ones((8, 256), F32),
+            gsend_wide, gbuf.at[:, 0, :, lane], g_ss.at[0], g_rs.at[0], ctx=c, tp=peer(k)
+        )
+
+    def row_sums(stream):
+        return lax.dot_general(
+            jnp.ones((8, stream.shape[1]), F32),
             stream * stream,
             NT,
             preferred_element_type=F32,
             precision=lax.Precision.HIGHEST,
         )
 
+    def spread_far():
+        arrived(rs_recv, p_rs)
+        stream = resid[...].astype(F32)
+        for k in range(8):
+            stream = stream + rs_recv[k].astype(F32)
+        gain = jnp.broadcast_to(gain_buf[...].astype(F32).reshape(1, 256), (128, 256))
+        scaled = (stream * gain).astype(BF16)
+        gsend[...] = scaled
+        g_cross().start()
+        for k in (2, 1, 3):
+            g_copy(k).start()
+        gbuf[t % 2, 1, :, lane] = scaled
+        far_squares[...] = row_sums(stream)
+        for k in range(1, 8):
+            sq_copy(k).start()
+
+    def swap_own():
+        arrived(ws_recv.at[1:4], w_rs)
+        stream = own[...]
+        for k in (1, 2, 3):
+            stream = stream + ws_recv[k].astype(F32)
+        swap_send[...] = stream.astype(BF16)
+        swap_copy().start()
+        own[...] = stream + resid_own[...].astype(F32)
+
+    def spread_own():
+        swap_copy().wait_recv()
+        stream = own[...] + swap_recv[...].astype(F32)
+        gain = jnp.broadcast_to(gain_wide[...].astype(F32).reshape(1, 512), (128, 512))
+        scaled = (stream * gain).astype(BF16)
+        gsend_wide[0] = scaled[:, 0:256]
+        gsend_wide[1] = scaled[:, 256:512]
+        for k in (2, 1, 3):
+            gw_copy(k).start()
+        gbuf[0, 0, :, lane] = scaled[:, 0:256]
+        gbuf[1, 0, :, lane] = scaled[:, 256:512]
+        own_squares[...] = row_sums(stream)
+        for k in (2, 1, 3):
+            oq_copy(k).start()
+
     def sq_copy(k):
-        return remote(sq_send, sq_recv.at[k], sq_ss.at[0], sq_rs.at[0], ctx=c, tp=(t + k) % 8)
+        return remote(far_squares, sq_recv.at[k], sq_ss.at[0], sq_rs.at[0], ctx=c, tp=(t + k) % 8)
+
+    def oq_copy(k):
+        return remote(own_squares, oq_recv.at[k], sq_ss.at[1], sq_rs.at[1], ctx=c, tp=peer(k))
 
     def sq_swap():
-        return remote(sq_recv.at[0, 1], sq_other, sq_ss.at[1], sq_rs.at[1], ctx=across, tp=t)
-
-    spread(1)
-    pass_on(3)
-    spread(0)
-    for k in range(1, 8):
-        sq_copy(k).start()
-    pass_on(4)
+        return remote(sq_recv.at[0], sq_other, sq_ss.at[2], sq_rs.at[2], ctx=across, tp=t)
+
+    for j in (6, 7):
+        pass_on(j)
+        direct_both(j + 5)
+    spread_far()
+    g_cross().wait_recv()
+    for k in (2, 1, 3):
+        g_forward(k).start()
+    swap_own()
+    pass_on(8)
+    direct_both(13)
     hand_over(0)
 
     def swap_squares():
         arrived(sq_recv.at[1:8], sq_rs.at[0])
-        for side in (1, 0):
-            squares = sq_send[side]
-            for k in range(1, 8):
-                squares = squares + sq_recv[k, side]
-            sq_recv[0, side] = squares
+        squares = far_squares[...]
+        for k in range(1, 8):
+            squares = squares + sq_recv[k]
+        sq_recv[0] = squares
         sq_swap().start()
 
-    def g_arrival(side):
-        arrived(rs_recv.at[0, 1:8], g_rs.at[side])
+    def find_scale():
+        sq_swap().wait_recv()
+        arrived(oq_recv.at[1:4], sq_rs.at[1])
+        squares = sq_other[...] + own_squares[...]
+        for k in (1, 2, 3):
+            squares = squares + oq_recv[k]
+        scale_row = lax.rsqrt(squares[0:1, :] * (1.0 / 4096.0) + 1e-05)
+        scale[...] = jnp.transpose(jnp.broadcast_to(scale_row, (128, 128)))
 
     def x_copy(j):
         return remote(xsend.at[j], xrecv.at[j], x_ss, x_rs.at[j], ctx=across, tp=t)
@@ -509,21 +608,29 @@
         left(q_all.at[1:8], q_ss)
         left(usend.at[1:8], u_ss)
         left(ssend.at[1:8], st_ss)
-        left(rs_send.at[1], p_ss.at[1])
-        for ref in (p_ss.at[0], g_ss.at[0], g_ss.at[1]):
-            left(rs_send.at[0, 1:8], ref)
+        left(rs_send, p_ss)
+        left(ws_send.at[1:4], w_ss)
+        swap_copy().wait_send()
+        left(ws_send.at[1:4], g_ss.at[0])
+        left(rs_send.at[0:6], g_ss.at[1])
+        g_cross().wait_send()
         left(sq_recv.at[1:8], sq_ss.at[0])
+        left(oq_recv.at[1:4], sq_ss.at[1])
         sq_swap().wait_send()
         left(wbuf.at[:, 0:512], d_ss)
         left(wbuf.at[:, 0:256], f_ss)
         left(wbuf.at[:, 0:1024], r_ss)
 
-    g_arrival(1)
+    arrived(rs_recv.at[0:6], g_rs.at[1])
 
     def chunk(j, _):
-        @pl.when(j < 2)
-        def _():
-            pass_on(j + 5)
+        for j_at, j_new in ((0, 9), (2, 10), (4, 11), (6, 12), (8, 13)):
+
+            @pl.when(j == j_at)
+            def _(j_new=j_new):
+                pass_on(j_new)
+
+        pl.when(j == 4)(swap_squares)
 
         @pl.when(j < CHUNKS - 1)
         def _():
@@ -533,35 +640,31 @@
         xsend[j] = half_product(j, 1).astype(BF16)
         x_copy(j).start()
 
-        @pl.when(j == 2)
-        def _():
-            g_arrival(0)
-            swap_squares()
-
-        @pl.when(j >= 2)
-        def _():
-            pown[j - 2] = half_product(j - 2, 0)
-
-        @pl.when(j == 4)
-        def _():
-            sq_swap().wait_recv()
-            squares = sq_recv[0, 0, 0:1, :] + sq_other[0:1, :]
-            scale_row = lax.rsqrt(squares * (1.0 / 4096.0) + 1e-05)
-            scale[...] = jnp.transpose(jnp.broadcast_to(scale_row, (128, 128)))
-
-        @pl.when(j >= 4)
-        def _():
-            finish(j - 4)
+        pl.when(j == 2)(spread_own)
+
+        @pl.when(j == LAG)
+        def _():
+            arrived(ws_recv.at[1:4], g_rs.at[0])
+
+        @pl.when(j >= LAG)
+        def _():
+            pown[j - LAG] = half_product(j - LAG, 0)
+
+        pl.when(j == 10)(find_scale)
+
+        @pl.when(j >= 10)
+        def _():
+            finish(j - 10)
 
         return 0
 
     lax.fori_loop(0, CHUNKS, chunk, 0)
+    for j in range(CHUNKS - LAG, CHUNKS):
+        pown[j] = half_product(j, 0)
+    for j in range(CHUNKS - 10, CHUNKS):
+        finish(j)
 
     drain()
-    for j in range(CHUNKS - 4, CHUNKS):
-        if j >= CHUNKS - 2:
-            pown[j] = half_product(j, 0)
-        finish(j)
     left(xsend, x_ss)
 
 
@@ -599,22 +702,32 @@
             V((1, 512), F32),
             V((1, 512), F32),
             V((128, 512), F32),
-            V((8, 512), F32),
+            V((2, 512), F32),
             V((8, 128), F32),
             V((8, 128, 512), BF16),
-            V((8, 8, 512), F32),
+            V((8, 2, 512), F32),
             V((4, 128, 512), BF16),
-            V((4, 8, 512), F32),
+            V((4, 2, 512), F32),
             V((4, 128, 512), BF16),
-            V((4, 8, 512), F32),
+            V((4, 2, 512), F32),
             V((16, 512, 256), BF16),
-            V((2, 128, 256), BF16),
+            V((128, 256), BF16),
+            V((128, 512), BF16),
             V((256,), BF16),
-            V((2, 8, 128, 256), BF16),
-            V((2, 8, 128, 256), BF16),
-            V((2, 8, 128), F32),
-            V((8, 2, 8, 128), F32),
+            V((512,), BF16),
+            V((8, 128, 256), BF16),
+            V((8, 128, 256), BF16),
+            V((4, 128, 512), BF16),
+            V((4, 128, 512), BF16),
+            V((128, 512), BF16),
+            V((128, 512), BF16),
+            V((128, 512), F32),
             V((8, 128), F32),
+            V((8, 128), F32),
+            V((8, 8, 128), F32),
+            V((4, 8, 128), F32),
+            V((8, 128), F32),
+            V((128, 256), BF16),
             V((2, 128, 256), BF16),
             V((2, 2, 128, 1024), BF16),
             V((CHUNKS, 2048, 2 * CW), BF16),
@@ -626,7 +739,7 @@
             dma((8,)),
             dma((4,)),
             dma((4,)),
-            dma((6,)),
+            dma((7,)),
             dma,
             dma,
             dma,
@@ -641,12 +754,16 @@
             dma((CHUNKS,)),
             dma,
             dma((CHUNKS,)),
-            dma((2,)),
-            dma((2,)),
-            dma((2,)),
-            dma((2,)),
-            dma((2,)),
-            dma((2,)),
+            dma,
+            dma,
+            dma,
+            dma,
+            dma,
+            dma,
+            dma((3,)),
+            dma((3,)),
+            dma((3,)),
+            dma((3,)),
             dma,
             dma((CHUNKS,)),
         ],

time: 94.9 us -> 89.8 us (0.946)
  Pallas kernels: 94 us -> 88.9 us
    pallas_call x1, Pallas kernels: 94 us -> 88.9 us  [body(): pl.pallas_call(kernel, out_shape=pltpu.VMEM((128, 1792), BF16), in_specs=...]
where the time goes in v4:
time: 89.8 us; the launch traced here: 89.7 us
  Pallas kernels  88.9 us (99%)
    pallas_call x1, Pallas kernels, body(): pl.pallas_call(kernel, out_shape=pltpu.VMEM((128, 1792), BF16), in_specs=...  88.9 us

profile of v4, /device:TPU:1, one launch (start us, length us, event | category | flops | bytes accessed | tf_op | source)
XLA Modules:
  0.0 89.7 jit_solution(8089171430585639936)
XLA Ops:
  0.0 88.9 %shard_map.109 = bf16[128,1792]{1,0:T(8,128)(2,1)S(1)} custom-call(bf16[128,512]{1,0:T(8,128)(2,1)} %q_hbm.1, bf16[2048,128]{1,0:T(8,128)(2,1)} %k_hbm.1, bf16[2048,128]{1,0:T(8,128)(2,1)} %v_hbm.1, s32[1,2]{1,0:T(1,128)} %bitcast.5, s32[16,128]{1,0:T(8,128)} %bitcast.3, s32[16,128]{1,0:T(8,128)} %bitcast.4, bf16[128,4096]{1,0:T(8,128)(2,1)} %resid_hbm.1, ...), custom_call_target="tpu_custom_call" | custom-call | flops 17999998976 | bytes 16000000 | tf_op jit(solution)/shard_map/pallas_call | solution.py:688
  88.9 0.8 copy.13

commit v5 on v4

--- a/solution.py
+++ b/solution.py
@@ -36,8 +36,8 @@
     q_hbm,
     k_hbm,
     v_hbm,
-    exps_ref,
-    qp_ref,
+    exps_hbm,
+    qp_hbm,
     kp_hbm,
     resid_hbm,
     ow_hbm,
@@ -49,6 +49,8 @@
     kbuf,
     vbuf,
     vt,
+    exps_ref,
+    qp_ref,
     kpraw,
     kposb,
     sa,
@@ -140,11 +142,28 @@
             src_ref=src, dst_ref=dst, send_sem=ss, recv_sem=rs, device_id=dev, device_id_type=MESH
         )
 
+    barrier = pltpu.get_barrier_semaphore()
+    peers = 0
+    for r in range(1, 8):
+        pl.semaphore_signal(
+            barrier, inc=1, device_id={"ctx": ctx_at(r // 4, r % 4), "tp": t}, device_id_type=MESH
+        )
+        pl.semaphore_signal(
+            barrier, inc=1, device_id={"ctx": c, "tp": (t + r) % 8}, device_id_type=MESH
+        )
+        pl.semaphore_signal(
+            barrier, inc=1, device_id={"ctx": across, "tp": (t + r) % 8}, device_id_type=MESH
+        )
+        peers += 3
+    pl.semaphore_signal(barrier, inc=1, device_id={"ctx": partner, "tp": t}, device_id_type=MESH)
+
     lq = pltpu.make_async_copy(q_hbm, q_all.at[0], loc_s.at[0])
     lk = pltpu.make_async_copy(k_hbm, kbuf.at[1], loc_s.at[1])
     lv = pltpu.make_async_copy(v_hbm, vbuf.at[1], loc_s.at[2])
     lp = pltpu.make_async_copy(kp_hbm, kpraw.at[1], loc_s.at[3])
-    for cp in (lq, lk, lv, lp):
+    lx = pltpu.make_async_copy(exps_hbm, exps_ref, loc_s.at[7])
+    lt = pltpu.make_async_copy(qp_hbm, qp_ref, loc_s.at[8])
+    for cp in (lq, lk, lv, lp, lx, lt):
         cp.start()
 
     own_rows = pl.multiple_of(core * 1024 + z * 256, 256)
@@ -161,38 +180,25 @@
         own_weight(j, 0).start()
         own_weight(j, 1).start()
 
-    barrier = pltpu.get_barrier_semaphore()
-    peers = 0
-    for r in range(1, 8):
-        pl.semaphore_signal(
-            barrier, inc=1, device_id={"ctx": ctx_at(r // 4, r % 4), "tp": t}, device_id_type=MESH
-        )
-        pl.semaphore_signal(
-            barrier, inc=1, device_id={"ctx": c, "tp": (t + r) % 8}, device_id_type=MESH
-        )
-        pl.semaphore_signal(
-            barrier, inc=1, device_id={"ctx": across, "tp": (t + r) % 8}, device_id_type=MESH
-        )
-        peers += 3
-    pl.semaphore_signal(barrier, inc=1, device_id={"ctx": partner, "tp": t}, device_id_type=MESH)
     pl.semaphore_wait(barrier, peers + 1)
 
     kv = [
-        remote(k_hbm, kbuf.at[0], kv_ss.at[0], kv_rs.at[0], ctx=partner, tp=t),
-        remote(v_hbm, vbuf.at[0], kv_ss.at[1], kv_rs.at[1], ctx=partner, tp=t),
-        remote(kp_hbm, kpraw.at[0], kv_ss.at[2], kv_rs.at[2], ctx=partner, tp=t),
+        remote(kbuf.at[1], kbuf.at[0], kv_ss.at[0], kv_rs.at[0], ctx=partner, tp=t),
+        remote(vbuf.at[1], vbuf.at[0], kv_ss.at[1], kv_rs.at[1], ctx=partner, tp=t),
+        remote(kpraw.at[1], kpraw.at[0], kv_ss.at[2], kv_rs.at[2], ctx=partner, tp=t),
     ]
 
     def q_copy(r):
         return remote(
-            q_hbm, q_all.at[r], q_ss, q_rs.at[r], ctx=ctx_at(r // 4, 4 - hop(r)), tp=t
-        )
-
-    kv[2].start()
-    for r in (1, 2, 4):
+            q_all.at[0], q_all.at[r], q_ss, q_rs.at[r], ctx=ctx_at(r // 4, 4 - hop(r)), tp=t
+        )
+
+    for cp in (lq, lk, lv, lp, lx, lt):
+        cp.wait()
+    for r in (2, 1, 4):
         q_copy(r).start()
-    kv[0].start()
-    kv[1].start()
+    for cp in kv:
+        cp.start()
 
     def q_pass(r):
         rows = pl.ds(pl.multiple_of(64 * (r - 1), 64), 64)
@@ -282,8 +288,6 @@
     cvec[...] = jnp.exp2(jnp.broadcast_to(exps_ref[0:1, 0:1], (8, 128)).astype(F32)) * BASE
     acc_u[...] = jnp.zeros_like(acc_u)
     acc_s[...] = jnp.zeros_like(acc_s)
-    for cp in (lq, lk, lv, lp):
-        cp.wait()
     prepare(1)
 
     def qk(i, j, buf, mref):
@@ -373,6 +377,7 @@
             @pl.when(i == 15)
             def _():
                 pass_on(3)
+                pass_on(4)
                 direct_both(6)
 
         @pl.when((odd == 0) & (i < 9))
@@ -418,7 +423,6 @@
 
     lax.fori_loop(1, 16, step, 0)
 
-    pass_on(4)
     direct_both(7)
     pass_on(5)
     for j in (8, 9, 10):
@@ -624,7 +628,7 @@
     arrived(rs_recv.at[0:6], g_rs.at[1])
 
     def chunk(j, _):
-        for j_at, j_new in ((0, 9), (2, 10), (4, 11), (6, 12), (8, 13)):
+        for j_at, j_new in ((1, 9), (3, 10), (5, 11), (7, 12), (9, 13)):
 
             @pl.when(j == j_at)
             def _(j_new=j_new):
@@ -688,13 +692,15 @@
     return pl.pallas_call(
         kernel,
         out_shape=pltpu.VMEM((128, 1792), BF16),
-        in_specs=[hbm, hbm, hbm, vmem, vmem, hbm, hbm, hbm, hbm, hbm, hbm],
+        in_specs=[hbm, hbm, hbm, hbm, hbm, hbm, hbm, hbm, hbm, hbm, hbm],
         out_specs=vmem,
         scratch_shapes=[
             V((8, 128, 512), BF16),
             V((2, 2048, 128), BF16),
             V((2, 2048, 128), BF16),
             V((2, 128, 2048), BF16),
+            V((1, 2), jnp.int32),
+            V((16, 128), jnp.int32),
             V((2, 16, 128), jnp.int32),
             V((2, 2048, 128), F32),
             V((KT, 512), F32),
@@ -739,7 +745,7 @@
             dma((8,)),
             dma((4,)),
             dma((4,)),
-            dma((7,)),
+            dma((9,)),
             dma,
             dma,
             dma,

time: 89.8 us -> 89.5 us (level)
  no operation moved by 1% of the time
where the time goes in v5:
time: 89.5 us; the launch traced here: 89.4 us
  Pallas kernels  88.6 us (99%)
    pallas_call x1, Pallas kernels, body(): pl.pallas_call(kernel, out_shape=pltpu.VMEM((128, 1792), BF16), in_specs=...  88.6 us

profile of v5, /device:TPU:1, one launch (start us, length us, event | category | flops | bytes accessed | tf_op | source)
XLA Modules:
  0.0 89.4 jit_solution(17346516323832198735)
XLA Ops:
  0.0 88.6 %shard_map.109 = bf16[128,1792]{1,0:T(8,128)(2,1)S(1)} custom-call(bf16[128,512]{1,0:T(8,128)(2,1)} %q_hbm.1, bf16[2048,128]{1,0:T(8,128)(2,1)} %k_hbm.1, bf16[2048,128]{1,0:T(8,128)(2,1)} %v_hbm.1, s32[1,2]{1,0:T(1,128)} %bitcast.5, s32[16,128]{1,0:T(8,128)} %bitcast.3, s32[16,128]{1,0:T(8,128)} %bitcast.4, bf16[128,4096]{1,0:T(8,128)(2,1)} %resid_hbm.1, ...), custom_call_target="tpu_custom_call" | custom-call | flops 17999998976 | bytes 16000000 | tf_op jit(solution)/shard_map/pallas_call | solution.py:692
  88.6 0.8 copy.13

commit v6 on v5

--- a/solution.py
+++ b/solution.py
@@ -384,9 +384,9 @@
         def _():
             direct_both(i // 2 + 1)
 
-        @pl.when((i == 4) | (i == 6) | (i == 9))
-        def _():
-            pass_on(i // 3 - 1)
+        @pl.when((i == 5) | (i == 7) | (i == 10))
+        def _():
+            pass_on((i - 4) // 2 - i // 10)
 
         pl.when(i == 7)(later_loads)
 

time: 89.5 us -> 89.4 us (level)
  no operation moved by 1% of the time
where the time goes in v6:
time: 89.4 us; the launch traced here: 89.3 us
  Pallas kernels  88.5 us (99%)
    pallas_call x1, Pallas kernels, body(): pl.pallas_call(kernel, out_shape=pltpu.VMEM((128, 1792), BF16), in_specs=...  88.5 us

profile of v6, /device:TPU:1, one launch (start us, length us, event | category | flops | bytes accessed | tf_op | source)
XLA Modules:
  0.0 89.3 jit_solution(17680082603565819143)
XLA Ops:
  0.0 88.5 %shard_map.109 = bf16[128,1792]{1,0:T(8,128)(2,1)S(1)} custom-call(bf16[128,512]{1,0:T(8,128)(2,1)} %q_hbm.1, bf16[2048,128]{1,0:T(8,128)(2,1)} %k_hbm.1, bf16[2048,128]{1,0:T(8,128)(2,1)} %v_hbm.1, s32[1,2]{1,0:T(1,128)} %bitcast.5, s32[16,128]{1,0:T(8,128)} %bitcast.3, s32[16,128]{1,0:T(8,128)} %bitcast.4, bf16[128,4096]{1,0:T(8,128)(2,1)} %resid_hbm.1, ...), custom_call_target="tpu_custom_call" | custom-call | flops 17999998976 | bytes 16000000 | tf_op jit(solution)/shard_map/pallas_call | solution.py:692
  88.5 0.8 copy.13
